TPU v7x, 256 devices: a whole 4x4x8 slice. The times are simulated.
256 devices in a mesh: seq: 4 (over y), expert: 64 (over x, z, core).
Axes of the slice: x: 4, y: 4, z: 8, core: 2. Of those that a mesh axis runs over, the one named last changes fastest.
Arguments:
- decoder_states: bfloat16 [64, 512, 1024], P('expert', 'seq'), may hold values from -8 to 8
- queries: bfloat16 [64, 512, 1024], P('expert', 'seq'), may hold values from -5 to 5
- encoder_keys: bfloat16 [64, 512, 1024], P('expert', 'seq'), may hold values from -5 to 5
- encoder_values: bfloat16 [64, 512, 1024], P('expert', 'seq'), may hold values from -6 to 6
- source_lengths: int32 [64], P('expert'), may hold values from 256 to 512
- norm_gain: float32 [1024], replicated, may hold values from 0.5 to 1.5
- router_weight: bfloat16 [1024, 64], replicated, may hold values from -0.1875 to 0.1875
- expert_ids: int32 [64, 512, 2], P('expert', 'seq'), may hold values from 0 to 63, all different within a row; in each aligned block of 128 rows (0 to 127, 128 to 255, ..., all dimensions but the last counted through in order) at most 6 rows name the same one
- expert_in: bfloat16 [64, 4096, 1024], P('expert', 'seq'), may hold values from -0.1875 to 0.1875
- expert_out: bfloat16 [64, 4096, 1024], P('expert', 'seq'), may hold values from -0.09375 to 0.09375
- grad_output: bfloat16 [64, 512, 1024], P('expert', 'seq'), may hold values from -6 to 6
Outputs:
- layer_output: bfloat16 [64, 512, 1024], P('expert', 'seq')
- grad_states: bfloat16 [64, 512, 1024], P('expert', 'seq')
- grad_queries: bfloat16 [64, 512, 1024], P('expert', 'seq')
- grad_keys: float32 [64, 512, 1024], P('expert', 'seq')
- grad_values: float32 [64, 512, 1024], P('expert', 'seq')
Inputs may be any that keep to these rules, and one draw needn't show every extreme that they name: `expert_ids`: the two experts of a position differ; among the 128 positions of one device (aligned blocks of the flattened sequence positions) no expert is named more than 6 times, a bound that some block reaches.
All inputs are finite; a program needn't handle non-finite values.
Results may differ from a plain program's by a relative error of at most 0.024.
Values may be sent and summed in bfloat16 or wider, within the bound.
A program may use at most 128 MiB of HBM per device.

v0:
```python
import math

import jax
import jax.numpy as jnp
from jax import lax
from jax.sharding import PartitionSpec as P

H = 8
HD = 128


gelu_scale = 0.7978845608028654
cubic_weight = 0.044715


def gelu_curve(signal):
    inner = gelu_scale * (signal + cubic_weight * signal * signal * signal)
    return 0.5 * signal * (1.0 + jnp.tanh(inner))


def gelu_slope(signal):
    tangent = jnp.tanh(gelu_scale * (signal + cubic_weight * signal * signal * signal))
    return 0.5 * (1.0 + tangent) + 0.5 * signal * (1.0 - tangent * tangent) * gelu_scale * (
        1.0 + 3.0 * cubic_weight * signal * signal
    )


def swap_experts(slot_block):
    return lax.all_to_all(slot_block, "expert", split_axis=0, concat_axis=0, tiled=True)


def gather_rows(matrix):
    return lax.all_gather(matrix, "seq", axis=0, tiled=True)


def reduce_rows(producer, row_count):
    return lax.psum_scatter(
        producer(jnp.int32(0), row_count * lax.axis_size("seq")).astype(jnp.bfloat16),
        "seq",
        scatter_dimension=0,
        tiled=True,
    ).astype(jnp.float32)


def on_device(
    decoder_states,
    queries,
    encoder_keys,
    encoder_values,
    source_lengths,
    norm_gain,
    router_weight,
    expert_ids,
    expert_in,
    expert_out,
    grad_output,
):
    token_count = decoder_states.shape[1]
    model_width = decoder_states.shape[2]
    expert_count = lax.axis_size("expert")
    capacity = max(2, 3 * token_count // expert_count)
    slot_count = expert_count * capacity
    score_scale = 1.0 / math.sqrt(HD)
    keys_all, values_all = (
        lax.all_gather(encoder_keys[0], "seq", axis=0, tiled=True),
        lax.all_gather(encoder_values[0], "seq", axis=0, tiled=True),
    )
    source_count = keys_all.shape[0]
    query_heads = queries[0].reshape(token_count, H, HD)
    key_heads = keys_all.reshape(source_count, H, HD)
    value_heads = values_all.reshape(source_count, H, HD)
    scores = (
        jnp.einsum("thd,khd->htk", query_heads, key_heads, preferred_element_type=jnp.float32)
        * score_scale
    )
    key_valid = lax.iota(jnp.int32, source_count) < source_lengths[0]
    scores = jnp.where(key_valid[None, None, :], scores, -1e30)
    row_max = jnp.max(scores, axis=-1, keepdims=True)
    raw_weights = jnp.exp(scores - row_max)
    probability = raw_weights / jnp.sum(raw_weights, axis=-1, keepdims=True)
    rounded_prob = probability.astype(jnp.bfloat16)
    context = jnp.einsum(
        "htk,khd->thd", rounded_prob, value_heads, preferred_element_type=jnp.float32
    ).reshape(token_count, model_width)
    residual = decoder_states[0].astype(jnp.float32) + context
    centred = residual - jnp.mean(residual, axis=-1, keepdims=True)
    reciprocal = 1.0 / jnp.sqrt(jnp.mean(centred * centred, axis=-1, keepdims=True) + 1e-05)
    normed = centred * reciprocal
    routed_in = (normed * norm_gain).astype(jnp.bfloat16)
    logits = jnp.dot(routed_in, router_weight, preferred_element_type=jnp.float32)
    chosen_experts = expert_ids[0]
    expert_iota = lax.iota(jnp.int32, expert_count)
    first_hot = chosen_experts[:, 0:1] == expert_iota[None, :]
    second_hot = chosen_experts[:, 1:2] == expert_iota[None, :]
    first_logit = jnp.sum(jnp.where(first_hot, logits, 0.0), axis=-1)
    second_logit = jnp.sum(jnp.where(second_hot, logits, 0.0), axis=-1)
    gates = jnp.stack(
        [
            1.0 / (1.0 + jnp.exp(second_logit - first_logit)),
            1.0 / (1.0 + jnp.exp(first_logit - second_logit)),
        ],
        axis=1,
    )
    pair_hot = (
        jnp.stack([first_hot, second_hot], axis=1)
        .reshape(2 * token_count, expert_count)
        .astype(jnp.int32)
    )
    running = jnp.cumsum(pair_hot, axis=0)
    slot_rank = (jnp.sum(running * pair_hot, axis=-1) - 1).reshape(token_count, 2)
    slot_index = chosen_experts * capacity + slot_rank
    slot_iota = lax.iota(jnp.int32, slot_count)
    pick_one = (slot_index[:, 0:1] == slot_iota[None, :]).astype(jnp.bfloat16)
    pick_two = (slot_index[:, 1:2] == slot_iota[None, :]).astype(jnp.bfloat16)
    send_rows = jnp.einsum(
        "tr,td->rd", pick_one + pick_two, routed_in, preferred_element_type=jnp.float32
    ).astype(jnp.bfloat16)
    cotangent = grad_output[0].astype(jnp.float32)
    slot_grad_one = (gates[:, 0:1] * cotangent).astype(jnp.bfloat16)
    slot_grad_two = (gates[:, 1:2] * cotangent).astype(jnp.bfloat16)
    grad_send = (
        jnp.einsum("tr,td->rd", pick_one, slot_grad_one, preferred_element_type=jnp.float32)
        + jnp.einsum("tr,td->rd", pick_two, slot_grad_two, preferred_element_type=jnp.float32)
    ).astype(jnp.bfloat16)
    arrived = swap_experts(send_rows.reshape(expert_count, capacity, model_width)).reshape(
        slot_count, model_width
    )
    gathered = gather_rows(arrived)
    hidden_in = jnp.einsum("rd,fd->rf", gathered, expert_in[0], preferred_element_type=jnp.float32)
    hidden = gelu_curve(hidden_in).astype(jnp.bfloat16)

    def project(first_row, row_count):
        return jnp.dot(hidden, expert_out[0], preferred_element_type=jnp.float32)

    expert_sum = reduce_rows(project, slot_count)
    back_rows = swap_experts(
        expert_sum.astype(jnp.bfloat16).reshape(expert_count, capacity, model_width)
    ).reshape(slot_count, model_width)
    grad_arrived = swap_experts(grad_send.reshape(expert_count, capacity, model_width)).reshape(
        slot_count, model_width
    )
    grad_gathered = gather_rows(grad_arrived)
    grad_hidden = (
        jnp.einsum("rd,fd->rf", grad_gathered, expert_out[0], preferred_element_type=jnp.float32)
        * gelu_slope(hidden_in)
    ).astype(jnp.bfloat16)

    def back_project(first_row, row_count):
        return jnp.dot(grad_hidden, expert_in[0], preferred_element_type=jnp.float32)

    grad_sum = reduce_rows(back_project, slot_count)
    grad_back = swap_experts(
        grad_sum.astype(jnp.bfloat16).reshape(expert_count, capacity, model_width)
    ).reshape(slot_count, model_width)
    out_one = jnp.dot(pick_one, back_rows, preferred_element_type=jnp.float32)
    out_two = jnp.dot(pick_two, back_rows, preferred_element_type=jnp.float32)
    layer_out = residual + gates[:, 0:1] * out_one + gates[:, 1:2] * out_two
    grad_routed = jnp.dot(pick_one, grad_back, preferred_element_type=jnp.float32) + jnp.dot(
        pick_two, grad_back, preferred_element_type=jnp.float32
    )
    gate_grads = jnp.stack(
        [jnp.sum(cotangent * out_one, axis=-1), jnp.sum(cotangent * out_two, axis=-1)], axis=1
    )
    gate_mean = jnp.sum(gates * gate_grads, axis=-1, keepdims=True)
    logit_parts = gates * (gate_grads - gate_mean)
    logit_grads = jnp.where(first_hot, logit_parts[:, 0:1], 0.0) + jnp.where(
        second_hot, logit_parts[:, 1:2], 0.0
    )
    grad_routed = grad_routed + jnp.dot(
        logit_grads, router_weight.astype(jnp.float32).T, precision=lax.Precision.HIGHEST
    )
    grad_norm = grad_routed * norm_gain
    grad_residual = cotangent + reciprocal * (
        grad_norm
        - jnp.mean(grad_norm, axis=-1, keepdims=True)
        - normed * jnp.mean(grad_norm * normed, axis=-1, keepdims=True)
    )
    grad_states = grad_residual.astype(jnp.bfloat16)
    grad_heads = grad_states.reshape(token_count, H, HD)
    grad_probability = jnp.einsum(
        "thd,khd->htk", grad_heads, value_heads, preferred_element_type=jnp.float32
    )
    row_inner = jnp.sum(probability * grad_probability, axis=-1, keepdims=True)
    grad_scores = (probability * (grad_probability - row_inner)).astype(jnp.bfloat16)
    grad_queries = (
        (
            jnp.einsum("htk,khd->thd", grad_scores, key_heads, preferred_element_type=jnp.float32)
            * score_scale
        )
        .reshape(token_count, model_width)
        .astype(jnp.bfloat16)
    )
    row_count = encoder_keys.shape[1] * lax.axis_size("seq")
    key_part = (
        jnp.einsum("htk,thd->khd", grad_scores, query_heads, preferred_element_type=jnp.float32)
        * score_scale
    )
    value_part = jnp.einsum(
        "htk,thd->khd", rounded_prob, grad_heads, preferred_element_type=jnp.float32
    )
    key_grads = lax.psum_scatter(
        jnp.concatenate(
            [key_part.reshape(row_count, model_width), value_part.reshape(row_count, model_width)],
            axis=1,
        ).astype(jnp.bfloat16),
        "seq",
        scatter_dimension=0,
        tiled=True,
    ).astype(jnp.float32)
    return (
        layer_out.astype(jnp.bfloat16)[None],
        grad_states[None],
        grad_queries[None],
        key_grads[:, :model_width][None],
        key_grads[:, model_width:][None],
    )


def solution(mesh):
    placed = (
        P("expert", "seq", None),
        P("expert", "seq", None),
        P("expert", "seq", None),
        P("expert", "seq", None),
        P("expert"),
        P(),
        P(),
        P("expert", "seq", None),
        P("expert", "seq", None),
        P("expert", "seq", None),
        P("expert", "seq", None),
    )
    return jax.shard_map(
        on_device,
        mesh=mesh,
        in_specs=placed,
        out_specs=(
            P("expert", "seq", None),
            P("expert", "seq", None),
            P("expert", "seq", None),
            P("expert", "seq", None),
            P("expert", "seq", None),
        ),
        check_vma=False,
    )
```

profile of v0, /device:TPU:1, one launch (start us, length us, event | category | flops | bytes accessed | tf_op | source)
XLA Modules:
  0.0 390.1 jit_solution(13532178243321689765)
XLA Ops:
  7.2 2.0 copy.64
  9.3 0.7 all-gather.13.cloned.1.call-update
  10.0 0.8 copy.69
  12.1 0.6 reduce-window.6
  13.4 1.1 copy.89
  14.9 26.9 %all-gather.11.cloned.1.call-done = bf16[1,512,1024]{1,2,0:T(8,128)(2,1)} async-done(((bf16[1,128,1024]{1,2,0:T(8,128)(2,1)}), bf16[1,512,1024]{1,2,0:T(8,128)(2,1)}) %all-gather.11.cloned.1.call-update) | async-done | bytes 1048592 | tf_op jit(solution)/shard_map/all_gather | solution.py:65
  41.8 3.4 fusion.82
  45.2 25.9 %all-gather.13.cloned.1.call-done = bf16[1,512,1024]{2,1,0:T(8,128)(2,1)} async-done(((bf16[1,128,1024]{2,1,0:T(8,128)(2,1)}), bf16[1,512,1024]{2,1,0:T(8,128)(2,1)}) %all-gather.13.cloned.1.call-update) | async-done | bytes 1048592 | tf_op jit(solution)/shard_map/all_gather | solution.py:66
  71.1 2.3 copy.67
  73.5 2.4 fusion.41
  76.6 1.4 convolution_convert_fusion.3
  78.0 2.2 reshape.251
  80.2 40.4 %all_to_all.20 = bf16[64,6,1024]{2,1,0:T(8,128)(2,1)} all-to-all(bf16[64,6,1024]{2,1,0:T(8,128)(2,1)} %reshape.251), channel_id=1, replica_groups=mesh['seq'=4,'expert'=64] {'expert'}, dimensions={0} | all-to-all | bytes 1572864 | tf_op jit(solution)/shard_map/all_to_all | solution.py:29
  120.6 2.2 reshape.252
  123.6 1.4 add_convert_fusion
  125.0 2.2 reshape.255
  127.2 34.8 %all_to_all.21 = bf16[64,6,1024]{2,1,0:T(8,128)(2,1)} all-to-all(bf16[64,6,1024]{2,1,0:T(8,128)(2,1)} %reshape.255), channel_id=1, replica_groups=mesh['seq'=4,'expert'=64] {'expert'}, dimensions={0} | all-to-all | bytes 1572864 | tf_op jit(solution)/shard_map/all_to_all | solution.py:29
  162.0 2.1 reshape.256
  164.5 5.6 %fusion.15 = f32[1536,1024]{1,0:T(8,128)S(1)} fusion(bf16[1536,1024]{1,0:T(8,128)(2,1)} %all-gather.7.cloned.1.call-done, bf16[1,1024,1024]{2,1,0:T(8,128)(2,1)S(1)} %copy-done), kind=kOutput, calls=%fused_computation.21 | convolution fusion | flops 3221225472 | bytes 11534336 | tf_op jit(solution)/shard_map/rd,fd->rf/dot_general | solution.py:129
  170.1 2.7 copy-done.25
  172.7 5.2 %convolution_convert_fusion.1 = bf16[1536,1024]{1,0:T(8,128)(2,1)} fusion(f32[1536,1024]{1,0:T(8,128)S(1)} %fusion.15, bf16[1,1024,1024]{2,1,0:T(8,128)(2,1)S(1)} %copy-done.24), kind=kOutput, calls=%fused_computation.12 | convolution fusion | flops 3236954112 | bytes 11534336 | tf_op jit(solution)/shard_map/dot_general | solution.py:133
  178.0 26.9 %all-gather.9.cloned.1.call-done = bf16[1536,1024]{1,0:T(8,128)(2,1)} async-done(((bf16[384,1024]{1,0:T(8,128)(2,1)}), bf16[1536,1024]{1,0:T(8,128)(2,1)}) %all-gather.9.cloned.1.call-update) | async-done | bytes 3145744 | tf_op jit(solution)/shard_map/all_gather | solution.py:33
  204.9 12.1 %convolution_convert_fusion = bf16[1536,1024]{1,0:T(8,128)(2,1)} fusion(bf16[1,1024,1024]{2,1,0:T(8,128)(2,1)S(1)} %copy-done, f32[1536,1024]{1,0:T(8,128)} %copy-done.25, bf16[1536,1024]{1,0:T(8,128)(2,1)} %all-gather.9.cloned.1.call-done, bf16[1,1024,1024]{2,1,0:T(8,128)(2,1)} %param.20), kind=kOutput, calls=%fused_computation.11 | convolution fusion | flops 6473908224 | bytes 16777216 | tf_op jit(solution)/shard_map/dot_general | solution.py:149
  217.1 31.4 %reduce-scatter.4.cloned.1.call-done = bf16[384,1024]{1,0:T(8,128)(2,1)} async-done(((bf16[1536,1024]{1,0:T(8,128)(2,1)}), bf16[384,1024]{1,0:T(8,128)(2,1)}) %reduce-scatter.4.cloned.1.call-update) | async-done | bytes 786448 | tf_op jit(solution)/shard_map/reduce_scatter | solution.py:37
  248.5 2.2 reshape.253
  250.6 10.8 %all-to-all-start.1 = ((bf16[64,6,1024]{2,1,0:T(8,128)(2,1)}), bf16[64,6,1024]{2,1,0:T(8,128)(2,1)}, u32[]{:S(2)}, u32[]{:S(2)}) async-start(bf16[64,6,1024]{2,1,0:T(8,128)(2,1)} %reshape.253), calls=%async_computation.2 | async-start | bytes 2097152 | tf_op jit(solution)/shard_map/all_to_all | solution.py:29
  261.4 30.0 %reduce-scatter.6.cloned.1.call-done = bf16[384,1024]{1,0:T(8,128)(2,1)} async-done(((bf16[1536,1024]{1,0:T(8,128)(2,1)}), bf16[384,1024]{1,0:T(8,128)(2,1)}) %reduce-scatter.6.cloned.1.call-update) | async-done | bytes 786448 | tf_op jit(solution)/shard_map/reduce_scatter | solution.py:37
  291.5 2.2 reshape.257
  293.7 10.8 %all-to-all-start.3 = ((bf16[64,6,1024]{2,1,0:T(8,128)(2,1)}), bf16[64,6,1024]{2,1,0:T(8,128)(2,1)}, u32[]{:S(2)}, u32[]{:S(2)}) async-start(bf16[64,6,1024]{2,1,0:T(8,128)(2,1)} %reshape.257), calls=%async_computation.5 | async-start | bytes 2097152 | tf_op jit(solution)/shard_map/all_to_all | solution.py:29
  304.7 1.4 reshape.254
  306.1 1.0 fusion.42
  307.2 2.1 fusion.27
  309.8 23.1 %all-to-all-done.3 = bf16[64,6,1024]{2,1,0:T(8,128)(2,1)} async-done(((bf16[64,6,1024]{2,1,0:T(8,128)(2,1)}), bf16[64,6,1024]{2,1,0:T(8,128)(2,1)}, u32[]{:S(2)}, u32[]{:S(2)}) %all-to-all-start.3) | async-done | bytes 786464 | tf_op jit(solution)/shard_map/all_to_all | solution.py:29
  332.9 1.4 reshape.258
  334.7 1.0 convolution_add_fusion.1
  335.8 1.3 fusion.81
  338.1 2.3 convolution_convert_fusion.2
  340.6 1.9 multiply_reduce_fusion
  342.4 1.3 copy.81
  343.8 2.6 multiply_convert_fusion.3
  346.4 1.4 multiply_convert_fusion.2
  347.8 2.3 copy.80
  350.1 3.1 pad_maximum_fusion
  353.2 1.7 fusion.21
  354.9 0.9 copy.82
  355.8 25.2 %reduce-scatter.8.cloned.1.call-done = bf16[128,2048]{1,0:T(8,128)(2,1)} async-done(((bf16[512,2048]{1,0:T(8,128)(2,1)}), bf16[128,2048]{1,0:T(8,128)(2,1)}) %reduce-scatter.8.cloned.1.call-update) | async-done | bytes 524304 | tf_op jit(solution)/shard_map/reduce_scatter | solution.py:201
  381.0 1.1 convert_element_type.114
  382.1 1.1 slice_bitcast_fusion
  (101 shorter events, 5.9 us)
Async XLA Ops:
  7.2 157.3 %copy-start = (bf16[1,1024,1024]{2,1,0:T(8,128)(2,1)S(1)}, bf16[1,1024,1024]{2,1,0:T(8,128)(2,1)}, u32[]{:S(2)}) copy-start(bf16[1,1024,1024]{2,1,0:T(8,128)(2,1)} %param.19) | copy-start | bytes 6291460
  7.2 7.3 %copy-start.1 = (bf16[1,128,1024]{2,1,0:T(8,128)(2,1)S(1)}, bf16[1,128,1024]{2,1,0:T(8,128)(2,1)}, u32[]{:S(2)}) copy-start(bf16[1,128,1024]{2,1,0:T(8,128)(2,1)} %param.11) | copy-start | bytes 786436
  7.2 34.6 %all-gather.11.cloned.1.call-start = ((), (), s32[]{:S(2)}) async-start(), calls=%async_computation.12 | async-start | bytes 1310720 | tf_op jit(solution)/shard_map/all_gather | solution.py:65
  9.2 61.9 %all-gather.13.cloned.1.call-start = ((), (), s32[]{:S(2)}) async-start(), calls=%async_computation.13 | async-start | bytes 1310720 | tf_op jit(solution)/shard_map/all_gather | solution.py:66
  10.0 154.5 %all-gather.7.cloned.1.call-start = ((), (), s32[]{:S(2)}) async-start(), calls=%async_computation.7 | async-start | bytes 3932160 | tf_op jit(solution)/shard_map/all_gather | solution.py:33
  11.0 111.8 %copy-start.16 = (s32[128]{0:T(128)}, s32[128]{0:T(128)S(1)}, u32[]{:S(2)}) copy-start(s32[128]{0:T(128)S(1)} %get-tuple-element.31) | copy-start | bytes 1540
  11.0 111.8 %copy-start.17 = (s32[128]{0:T(128)}, s32[128]{0:T(128)S(1)}, u32[]{:S(2)}) copy-start(s32[128]{0:T(128)S(1)} %get-tuple-element.32) | copy-start | bytes 1540
  14.5 58.9 %copy-start.6 = (bf16[1,128,1024]{1,2,0:T(8,128)(2,1)}, bf16[1,128,1024]{1,2,0:T(8,128)(2,1)S(1)}, u32[]{:S(2)}) copy-start(bf16[1,128,1024]{1,2,0:T(8,128)(2,1)S(1)} %copy.89) | copy-start | bytes 786436
  14.9 61.6 %copy-start.12 = (s32[128]{0:T(128)}, s32[128]{0:T(128)S(1)}, u32[]{:S(2)}) copy-start(s32[128]{0:T(128)S(1)} %get-tuple-element.30) | copy-start | bytes 1540
  45.2 30.7 %copy-start.20 = (f32[8,128]{1,0:T(8,128)}, f32[8,128]{1,0:T(8,128)S(1)}, u32[]{:S(2)}) copy-start(f32[8,128]{1,0:T(8,128)S(1)} %get-tuple-element.42) | copy-start | bytes 12292
  73.5 2.8 copy-start.11
  75.9 0.6 copy-start.14
  76.1 0.5 copy-start.18
  78.0 44.9 %copy-start.10 = (bf16[1024,64]{0,1:T(8,128)(2,1)S(1)}, bf16[1024,64]{0,1:T(8,128)(2,1)}, u32[]{:S(2)}) copy-start(bf16[1024,64]{0,1:T(8,128)(2,1)} %param.17) | copy-start | bytes 393220
  78.0 45.1 %copy-start.3 = (bf16[1,128,1024]{2,1,0:T(8,128)(2,1)S(1)}, bf16[1,128,1024]{2,1,0:T(8,128)(2,1)}, u32[]{:S(2)}) copy-start(bf16[1,128,1024]{2,1,0:T(8,128)(2,1)} %param.21) | copy-start | bytes 786436
  80.2 43.4 %copy-start.13 = (s32[128]{0:T(128)S(1)}, s32[128]{0:T(128)}, u32[]{:S(2)}) copy-start(s32[128]{0:T(128)} %copy-done.12) | copy-start | bytes 1540
  122.8 82.2 %all-gather.9.cloned.1.call-start = ((), (), s32[]{:S(2)}) async-start(), calls=%async_computation.9 | async-start | bytes 3932160 | tf_op jit(solution)/shard_map/all_gather | solution.py:33
  164.2 84.3 %reduce-scatter.4.cloned.1.call-start = ((), (), s32[]{:S(2)}) async-start(), calls=%async_computation.8 | async-start | bytes 3932160 | tf_op jit(solution)/shard_map/reduce_scatter | solution.py:37
  164.5 8.3 %copy-start.24 = (bf16[1,1024,1024]{2,1,0:T(8,128)(2,1)S(1)}, bf16[1,1024,1024]{2,1,0:T(8,128)(2,1)}, u32[]{:S(2)}) copy-start(bf16[1,1024,1024]{2,1,0:T(8,128)(2,1)} %param.20) | copy-start | bytes 6291460
  170.1 2.7 copy-start.25
  177.9 113.5 %reduce-scatter.6.cloned.1.call-start = ((), (), s32[]{:S(2)}) async-start(), calls=%async_computation.10 | async-start | bytes 3932160 | tf_op jit(solution)/shard_map/reduce_scatter | solution.py:37
  250.6 43.0 %all-to-all-start.1 = ((bf16[64,6,1024]{2,1,0:T(8,128)(2,1)}), bf16[64,6,1024]{2,1,0:T(8,128)(2,1)}, u32[]{:S(2)}, u32[]{:S(2)}) async-start(bf16[64,6,1024]{2,1,0:T(8,128)(2,1)} %reshape.253), calls=%async_computation.2 | async-start | bytes 2097152 | tf_op jit(solution)/shard_map/all_to_all | solution.py:29
  293.7 39.3 %all-to-all-start.3 = ((bf16[64,6,1024]{2,1,0:T(8,128)(2,1)}), bf16[64,6,1024]{2,1,0:T(8,128)(2,1)}, u32[]{:S(2)}, u32[]{:S(2)}) async-start(bf16[64,6,1024]{2,1,0:T(8,128)(2,1)} %reshape.257), calls=%async_computation.5 | async-start | bytes 2097152 | tf_op jit(solution)/shard_map/all_to_all | solution.py:29
  304.5 76.5 %reduce-scatter.8.cloned.1.call-start = ((), (), s32[]{:S(2)}) async-start(), calls=%async_computation.11 | async-start | bytes 2621440 | tf_op jit(solution)/shard_map/reduce_scatter | solution.py:201
  309.8 27.3 %copy-start.15 = (f32[128]{0:T(128)S(1)}, f32[128]{0:T(128)}, u32[]{:S(2)}) copy-start(f32[128]{0:T(128)} %copy-done.14) | copy-start | bytes 1540
  309.8 27.3 %copy-start.19 = (f32[128]{0:T(128)S(1)}, f32[128]{0:T(128)}, u32[]{:S(2)}) copy-start(f32[128]{0:T(128)} %copy-done.18) | copy-start | bytes 1540
  334.3 1.4 copy-start.2
  334.4 1.4 copy-start.22
  334.4 1.4 copy-start.23
  334.4 2.8 copy-start.4
  334.7 3.4 copy-start.21
  337.4 0.7 copy-start.9
  338.1 2.3 copy-start.5
  338.1 2.5 copy-start.8
  343.8 2.6 copy-start.7
Sparse Core Ops, SparseCore 0:
  10.4 31.3 all-gather.10
  43.6 27.4 all-gather.12
  122.9 37.9 all-gather.6
  164.3 40.5 all-gather.8
  207.3 41.0 reduce-scatter.3
  250.9 40.5 reduce-scatter.5
  353.4 27.5 reduce-scatter.7
where the time goes:
time: 391 us; the launch traced here: 390 us
  waiting for transfers between devices  190 us (49%)
  blocking collectives  75.2 us (19%)
  matrix products  45.1 us (12%)
  local copies, waits for them, and re-layouts  33.3 us (9%)
  starting transfers between devices  22.3 us (6%)
  between operations  15.3 us (4%)
  other arithmetic  8.38 us (2%)
    all_to_all x2, blocking collectives, swap_experts(): lax.all_to_all(slot_block, 'expert', split_axis=0, concat_axis=0, tiled=T...  75.2 us
    reduce_scatter x2, waiting for transfers between devices, reduce_rows(): lax.psum_scatter(producer(jnp.int32(0), row_count * lax.axis_size('seq'))...  61.4 us
    all_gather x2, waiting for transfers between devices, gather_rows(): return lax.all_gather(matrix, 'seq', axis=0, tiled=True)  27 us
    all_gather x1, waiting for transfers between devices, on_device(): lax.all_gather(encoder_keys[0], 'seq', axis=0, tiled=True)  26.9 us
    all_gather x1, waiting for transfers between devices, on_device(): lax.all_gather(encoder_values[0], 'seq', axis=0, tiled=True)  25.9 us
    reduce_scatter x1, waiting for transfers between devices, on_device(): lax.psum_scatter(jnp.concatenate([key_part.reshape(row_count, model_width...  25.2 us
    all_to_all x2, waiting for transfers between devices, swap_experts(): lax.all_to_all(slot_block, 'expert', split_axis=0, concat_axis=0, tiled=T...  23.1 us
    all_to_all x2, starting transfers between devices, swap_experts(): lax.all_to_all(slot_block, 'expert', split_axis=0, concat_axis=0, tiled=T...  21.6 us
  transfers between devices with their start and end apart: 9, of which 7 were waited for; matrix products, arithmetic and copies ran while one was open for 12% of the time, Pallas kernels for 0%

commit v1 on v0

v1 whole, which is shorter than its diff:
```python
import functools
import math

import jax
import jax.numpy as jnp
import numpy as np
from jax import lax
from jax.experimental import pallas as pl
from jax.experimental.pallas import tpu as pltpu
from jax.sharding import PartitionSpec as P

H = 8
HD = 128
CAP = 6
SIDE = 8
GROUP = SIDE * CAP
SLOTS = SIDE * GROUP
MESH = pl.DeviceIdType.MESH
F32 = jnp.float32
BF16 = jnp.bfloat16

gelu_scale = 0.7978845608028654
cubic_weight = 0.044715

KV, GR, XR = 0, 1, 2
RG, RO, RKV = 0, 1, 2
AG, AX, BG, BO = 0, 1, 2, 3


def dot_nn(a, b):
    return lax.dot_general(a, b, (((1,), (0,)), ((), ())), preferred_element_type=F32)


def dot_nt(a, b):
    return lax.dot_general(a, b, (((1,), (1,)), ((), ())), preferred_element_type=F32)


def dot_tn(a, b):
    return lax.dot_general(a, b, (((0,), (0,)), ((), ())), preferred_element_type=F32)


def layer(
    length_ref,
    dec_ref,
    q_ref,
    k_ref,
    v_ref,
    gain_ref,
    router_ref,
    ids_ref,
    win_ref,
    wout_ref,
    gout_ref,
    swap_ref,
    layer_ref,
    gstates_ref,
    gq_ref,
    gk_ref,
    gv_ref,
    kvb,
    win,
    wout,
    xg,
    gg,
    send,
    zbuf,
    turned,
    pick,
    prob,
    residual,
    normed,
    hid,
    ghd,
    part,
    opp,
    near_l,
    near_r,
    kpart,
    kopp,
    knear_l,
    knear_r,
    back_x,
    local_sem,
    ag_s,
    ag_r,
    rs_s,
    rs_r,
    xs_s,
    xs_r,
):
    tokens, width = dec_ref.shape
    half = width // 2
    ny = lax.axis_size("seq")
    y = lax.axis_index("seq")
    e = lax.axis_index("expert")
    core = lax.rem(e, 2)
    z = lax.rem(e // 2, SIDE)
    x = e // (2 * SIDE)
    xc = x * 2 + core
    right = (lax.rem(y + 1, ny), e)
    left = (lax.rem(y + ny - 1, ny), e)
    hops = (4, 3, 5, 2, 6, 1, 7)

    def z_peer(hop):
        there = lax.rem(z + hop, SIDE)
        return there, (y, x * (2 * SIDE) + there * 2 + core)

    def xc_peer(hop):
        there = lax.rem(xc + hop, SIDE)
        return there, (y, (there // 2) * (2 * SIDE) + z * 2 + lax.rem(there, 2))

    def remote(src, dst, s, r, device):
        return pltpu.make_async_remote_copy(
            src_ref=src, dst_ref=dst, send_sem=s, recv_sem=r, device_id=device, device_id_type=MESH
        )

    own_k = pltpu.make_async_copy(k_ref, kvb.at[0, 0], local_sem.at[0])
    own_v = pltpu.make_async_copy(v_ref, kvb.at[0, 1], local_sem.at[1])
    own_in = pltpu.make_async_copy(win_ref, win, local_sem.at[2])
    own_out = pltpu.make_async_copy(wout_ref, wout, local_sem.at[3])
    for copy in (own_k, own_v, own_in, own_out):
        copy.start()

    barrier = pltpu.get_barrier_semaphore()
    for device in (left, right):
        pl.semaphore_signal(barrier, inc=1, device_id=device, device_id_type=MESH)
    for hop in hops:
        pl.semaphore_signal(barrier, inc=1, device_id=z_peer(hop)[1], device_id_type=MESH)
        pl.semaphore_signal(barrier, inc=1, device_id=xc_peer(hop)[1], device_id_type=MESH)
    pl.semaphore_wait(barrier, 2 + 2 * len(hops))

    class Gather:
        def __init__(self, number, buf, sources):
            def at(i):
                return ag_s.at[number * 6 + i], ag_r.at[number * 6 + i]

            self.to_right = [remote(sources[h], buf.at[3, h], *at(h), right) for h in (0, 1)]
            self.to_left = [remote(sources[h], buf.at[1, h], *at(2 + h), left) for h in (0, 1)]
            self.on_right = remote(buf.at[3, 0], buf.at[2, 0], *at(4), right)
            self.on_left = remote(buf.at[1, 1], buf.at[2, 1], *at(5), left)

        def forward_right(self):
            self.to_right[0].wait_recv()
            self.on_right.start()

        def forward_left(self):
            self.to_left[1].wait_recv()
            self.on_left.start()

        def sent(self):
            for copy in (*self.to_right, *self.to_left, self.on_right, self.on_left):
                copy.wait_send()

    class Reduce:
        def __init__(self, number, parts, across, from_left, from_right):
            def at(i):
                return rs_s.at[number * 6 + i], rs_r.at[number * 6 + i]

            self.parts, self.across = parts, across
            self.left_a = remote(parts.at[3, 0], from_right.at[0], *at(0), left)
            self.right_b = remote(parts.at[1, 1], from_left.at[1], *at(1), right)
            self.opposite_a = remote(parts.at[2, 0], across.at[0], *at(2), right)
            self.opposite_b = remote(parts.at[2, 1], across.at[1], *at(3), left)
            self.right_a = remote(parts.at[1, 0], from_left.at[0], *at(4), right)
            self.left_b = remote(parts.at[3, 1], from_right.at[1], *at(5), left)

        def pass_on(self):
            self.opposite_a.wait_recv()
            self.parts[1, 0] = (self.parts[1, 0].astype(F32) + self.across[0].astype(F32)).astype(BF16)
            self.right_a.start()
            self.opposite_b.wait_recv()
            self.parts[3, 1] = (self.parts[3, 1].astype(F32) + self.across[1].astype(F32)).astype(BF16)
            self.left_b.start()

        def arrived(self):
            for copy in (self.left_a, self.right_b, self.right_a, self.left_b):
                copy.wait_recv()

        def sent(self):
            for copy in (self.left_a, self.right_b, self.opposite_a, self.opposite_b, self.right_a, self.left_b):
                copy.wait_send()

    class Stage:
        def __init__(self, number, src, dst, peer, mine):
            self.s, self.r = xs_s.at[number], xs_r.at[number]
            self.src, self.dst, self.peer, self.mine = src, dst, peer, mine

        def rows(self, at):
            return pl.ds(pl.multiple_of(at * GROUP, 16), GROUP)

        def start(self):
            own = self.rows(self.mine)
            for hop in hops:
                there, device = self.peer(hop)
                remote(self.src.at[self.rows(there)], self.dst.at[own], self.s, self.r, device).start()
            pltpu.make_async_copy(self.src.at[own], self.dst.at[own], self.r).start()

        def arrived(self):
            pltpu.make_async_copy(self.src, self.dst, self.r).wait()

        def sent(self):
            most = pl.ds(0, SLOTS - GROUP)
            remote(self.src.at[most], self.dst.at[most], self.s, self.r, right).wait_send()

    def turn(src, dst):
        dst[...] = dot_nn(swap_ref[...], src[...]).astype(BF16)

    class Dispatch:
        def __init__(self, number, tensor, dst):
            self.first = [Stage(number * 4 + h, send.at[tensor, h], zbuf.at[tensor, h], z_peer, z) for h in (0, 1)]
            self.second = [Stage(number * 4 + 2 + h, turned.at[tensor, h], dst.at[h], xc_peer, xc) for h in (0, 1)]
            self.tensor = tensor

        def middle(self, h):
            self.first[h].arrived()
            turn(zbuf.at[self.tensor, h], turned.at[self.tensor, h])
            self.second[h].start()

        def sent(self):
            for stage in (*self.first, *self.second):
                stage.sent()

    class Return:
        def __init__(self, number, tensor, dst):
            self.first = [Stage(number * 4 + h, send.at[tensor, h], zbuf.at[tensor, h], xc_peer, xc) for h in (0, 1)]
            self.second = [Stage(number * 4 + 2 + h, turned.at[tensor, h], dst.at[h], z_peer, z) for h in (0, 1)]
            self.tensor = tensor

        middle = Dispatch.middle
        sent = Dispatch.sent

    keys = Gather(KV, kvb, (k_ref, v_ref))
    keys.to_right[0].start()
    keys.to_left[1].start()
    keys.to_right[1].start()
    keys.to_left[0].start()

    ids = ids_ref[...]
    experts = router_ref.shape[1]
    lanes = lax.broadcasted_iota(jnp.int32, (tokens, experts), 1)
    first_hot = ids[:, 0:1] == lanes
    second_hot = ids[:, 1:2] == lanes
    ones = first_hot.astype(F32), second_hot.astype(F32)
    earlier = (
        lax.broadcasted_iota(jnp.int32, (tokens, tokens), 0) > lax.broadcasted_iota(jnp.int32, (tokens, tokens), 1)
    ).astype(F32).astype(BF16)
    slot_lanes = lax.broadcasted_iota(jnp.int32, (tokens, SLOTS), 1)
    base = ((lanes // 2) % SIDE) * GROUP + (lanes // (2 * SIDE)) * (2 * CAP) + (lanes % 2) * CAP
    both = jnp.zeros((tokens, SLOTS), F32)
    for j in (0, 1):
        rank = dot_nn(earlier, ones[j].astype(BF16))
        if j == 1:
            rank = rank + jnp.sum(ones[0], axis=0, keepdims=True)
        slot = jnp.sum(ones[j] * (rank + base.astype(F32)), axis=-1, keepdims=True)
        chosen = (slot.astype(jnp.int32) == slot_lanes).astype(F32)
        pick[j] = chosen.astype(BF16)
        both = both + chosen
    spread = both.T.astype(BF16)
    for h in (0, 1):
        send[0, h] = dot_nn(spread, gout_ref[:, h * half : (h + 1) * half]).astype(BF16)

    grads = Dispatch(AG, 0, gg.at[0])
    grads.first[0].start()
    grads.first[1].start()
    keys.forward_right()
    keys.forward_left()
    grads.middle(0)
    grads.middle(1)
    keys.to_right[1].wait_recv()
    keys.to_left[0].wait_recv()
    own_k.wait()
    own_v.wait()
    keys.on_right.wait_recv()
    keys.on_left.wait_recv()

    score_scale = 1.0 / math.sqrt(HD)
    block_rows = kvb.shape[2]
    sources = ny * block_rows
    place = lax.broadcasted_iota(jnp.int32, (tokens, sources), 1)
    place = (place // block_rows + y) % ny * block_rows + place % block_rows
    valid = place < length_ref[0]

    def columns(head):
        return pl.ds(pl.multiple_of(head * HD, HD), HD)

    def attend(head, carry):
        at = columns(head)
        key_rows = kvb[:, 0, :, at].reshape(sources, HD)
        scores = dot_nt(q_ref[:, at], key_rows) * score_scale
        scores = jnp.where(valid, scores, -1e30)
        raw = jnp.exp(scores - jnp.max(scores, axis=-1, keepdims=True))
        probability = raw / jnp.sum(raw, axis=-1, keepdims=True)
        prob[head] = probability
        value_rows = kvb[:, 1, :, at].reshape(sources, HD)
        residual[:, at] = dec_ref[:, at].astype(F32) + dot_nn(probability.astype(BF16), value_rows)
        return carry

    lax.fori_loop(0, H, attend, 0)

    grad_rows = Gather(GR, gg, (gg.at[0, 0], gg.at[0, 1]))
    for h in (0, 1):
        grads.second[h].arrived()
        grad_rows.to_right[h].start()
        grad_rows.to_left[h].start()

    whole = residual[...]
    centred = whole - jnp.mean(whole, axis=-1, keepdims=True)
    reciprocal = 1.0 / jnp.sqrt(jnp.mean(centred * centred, axis=-1, keepdims=True) + 1e-05)
    normed[...] = centred * reciprocal
    routed_in = (normed[...] * gain_ref[...]).astype(BF16)
    for h in (0, 1):
        send[1, h] = dot_nn(spread, routed_in[:, h * half : (h + 1) * half]).astype(BF16)
    rows = Dispatch(AX, 1, xg.at[0])
    rows.first[0].start()
    rows.first[1].start()

    logits = dot_nn(routed_in, router_ref[...])
    first_logit = jnp.sum(jnp.where(first_hot, logits, 0.0), axis=-1, keepdims=True)
    second_logit = jnp.sum(jnp.where(second_hot, logits, 0.0), axis=-1, keepdims=True)
    gates = 1.0 / (1.0 + jnp.exp(second_logit - first_logit)), 1.0 / (1.0 + jnp.exp(first_logit - second_logit))

    grad_rows.forward_right()
    rows.middle(0)
    grad_rows.forward_left()
    rows.middle(1)
    row_gather = Gather(XR, xg, (xg.at[0, 0], xg.at[0, 1]))
    for h in (0, 1):
        rows.second[h].arrived()
        row_gather.to_right[h].start()
        row_gather.to_left[h].start()
    own_in.wait()
    own_out.wait()
    grad_rows.to_right[1].wait_recv()
    grad_rows.to_left[0].wait_recv()

    hidden_units = win.shape[0]
    step = 256

    def expert(d):
        def up(i, carry):
            at = pl.ds(pl.multiple_of(i * step, step), step)
            weight_in, weight_out = win[at, :], wout[at, :]
            signal = dot_nt(xg[d, 0], weight_in[:, :half]) + dot_nt(xg[d, 1], weight_in[:, half:])
            cotangent = dot_nt(gg[d, 0], weight_out[:, :half]) + dot_nt(gg[d, 1], weight_out[:, half:])
            square = signal * signal
            tangent = jnp.tanh(gelu_scale * (signal + cubic_weight * signal * square))
            upper = 0.5 * (1.0 + tangent)
            hid[:, at] = (signal * upper).astype(BF16)
            slope = upper + 0.5 * signal * (1.0 - tangent * tangent) * gelu_scale * (1.0 + 3.0 * cubic_weight * square)
            ghd[:, at] = (cotangent * slope).astype(BF16)
            return carry

        lax.fori_loop(0, hidden_units // step, up, 0)
        for n in range(width // step):
            at = slice(n * step, (n + 1) * step)
            h, low = divmod(n * step, half)
            inner = slice(low, low + step)
            part[0, d, h, :, inner] = dot_nn(ghd[...], win[:, at]).astype(BF16)
            part[1, d, h, :, inner] = dot_nn(hid[...], wout[:, at]).astype(BF16)

    sums = [Reduce(i, part.at[i], opp.at[i], near_l.at[i], near_r.at[i]) for i in (RG, RO)]
    expert(0)
    row_gather.forward_right()
    row_gather.forward_left()
    row_gather.to_right[1].wait_recv()
    expert(3)
    for total in sums:
        total.left_a.start()
    row_gather.to_left[0].wait_recv()
    expert(1)
    for total in sums:
        total.right_b.start()
    grad_rows.on_right.wait_recv()
    grad_rows.on_left.wait_recv()
    row_gather.on_right.wait_recv()
    row_gather.on_left.wait_recv()
    expert(2)
    for total in sums:
        total.opposite_a.start()
        total.opposite_b.start()
    for total in sums:
        total.pass_on()
    returns = []
    for i in (RG, RO):
        sums[i].arrived()
        back = Return((BG, BO)[i], 2 + i, back_x.at[i])
        for h in (0, 1):
            send[2 + i, h] = (
                part[i, 0, h].astype(F32) + near_l[i, h].astype(F32) + near_r[i, h].astype(F32)
            ).astype(BF16)
            back.first[h].start()
        returns.append(back)
    for back in returns:
        back.middle(0)
        back.middle(1)
    for back in returns:
        back.second[0].arrived()
        back.second[1].arrived()

    outs, grad_routed = [], None
    for j in (0, 1):
        outs.append(jnp.concatenate([dot_nn(pick[j], back_x[1, h]) for h in (0, 1)], axis=1))
        grad = gates[j] * jnp.concatenate([dot_nn(pick[j], back_x[0, h]) for h in (0, 1)], axis=1)
        grad_routed = grad if grad_routed is None else grad_routed + grad
    layer_ref[...] = (residual[...] + gates[0] * outs[0] + gates[1] * outs[1]).astype(BF16)
    cotangent = gout_ref[...].astype(F32)
    gate_grads = [jnp.sum(cotangent * out, axis=-1, keepdims=True) for out in outs]
    gate_mean = gates[0] * gate_grads[0] + gates[1] * gate_grads[1]
    parts = [gates[j] * (gate_grads[j] - gate_mean) for j in (0, 1)]
    rest = jnp.where(first_hot, parts[0], 0.0) + jnp.where(second_hot, parts[1], 0.0)
    for _ in range(3):
        piece = rest.astype(BF16)
        grad_routed = grad_routed + dot_nt(piece, router_ref[...])
        rest = rest - piece.astype(F32)
    grad_norm = grad_routed * gain_ref[...]
    state = normed[...]
    grad_states = cotangent + reciprocal * (
        grad_norm
        - jnp.mean(grad_norm, axis=-1, keepdims=True)
        - state * jnp.mean(grad_norm * state, axis=-1, keepdims=True)
    )
    gstates_ref[...] = grad_states.astype(BF16)

    def attend_back(head, carry):
        at = columns(head)
        key_rows = kvb[:, 0, :, at].reshape(sources, HD)
        value_rows = kvb[:, 1, :, at].reshape(sources, HD)
        probability = prob[head]
        grad_head = gstates_ref[:, at]
        grad_probability = dot_nt(grad_head, value_rows)
        inner = jnp.sum(probability * grad_probability, axis=-1, keepdims=True)
        grad_scores = (probability * (grad_probability - inner)).astype(BF16)
        gq_ref[:, at] = (dot_nn(grad_scores, key_rows) * score_scale).astype(BF16)
        key_part = (dot_tn(grad_scores, q_ref[:, at]) * score_scale).astype(BF16)
        value_part = dot_tn(probability.astype(BF16), grad_head).astype(BF16)
        kpart[:, 0, :, at] = key_part.reshape(ny, block_rows, HD)
        kpart[:, 1, :, at] = value_part.reshape(ny, block_rows, HD)
        return carry

    lax.fori_loop(0, H, attend_back, 0)
    key_sum = Reduce(RKV, kpart, kopp, knear_l, knear_r)
    key_sum.opposite_a.start()
    key_sum.opposite_b.start()
    key_sum.right_b.start()
    key_sum.left_a.start()
    key_sum.pass_on()
    key_sum.arrived()
    for h, out in ((0, gk_ref), (1, gv_ref)):
        out[...] = kpart[0, h].astype(F32) + knear_l[h].astype(F32) + knear_r[h].astype(F32)

    for gather in (keys, grad_rows, row_gather):
        gather.sent()
    for total in (*sums, key_sum):
        total.sent()
    for exchange in (grads, rows, *returns):
        exchange.sent()


def swap_matrix():
    at = np.arange(SLOTS)
    outer, middle, inner = at // GROUP, at % GROUP // CAP, at % CAP
    matrix = np.zeros((SLOTS, SLOTS), np.float32)
    matrix[at, middle * GROUP + outer * CAP + inner] = 1.0
    return matrix


def on_device(dec, q, k, v, lengths, gain, router, ids, win, wout, gout):
    tokens, width = dec.shape[1:]
    block_rows = k.shape[1]
    hidden_units = win.shape[1]
    half = width // 2
    vmem = pl.BlockSpec(memory_space=pltpu.VMEM)
    hbm = pl.BlockSpec(memory_space=pl.ANY)
    shape = jax.ShapeDtypeStruct
    rows = (2, SLOTS, half)
    outs = pl.pallas_call(
        layer,
        out_shape=(
            shape((tokens, width), BF16),
            shape((tokens, width), BF16),
            shape((tokens, width), BF16),
            shape((block_rows, width), F32),
            shape((block_rows, width), F32),
        ),
        in_specs=[
            pl.BlockSpec(memory_space=pltpu.SMEM),
            vmem,
            vmem,
            hbm,
            hbm,
            vmem,
            vmem,
            vmem,
            hbm,
            hbm,
            vmem,
            vmem,
        ],
        out_specs=[vmem] * 5,
        scratch_shapes=[
            pltpu.VMEM((4, 2, block_rows, width), BF16),
            pltpu.VMEM((hidden_units, width), BF16),
            pltpu.VMEM((hidden_units, width), BF16),
            pltpu.VMEM((4, *rows), BF16),
            pltpu.VMEM((4, *rows), BF16),
            pltpu.VMEM((4, *rows), BF16),
            pltpu.VMEM((4, *rows), BF16),
            pltpu.VMEM((4, *rows), BF16),
            pltpu.VMEM((2, tokens, SLOTS), BF16),
            pltpu.VMEM((H, tokens, 4 * block_rows), F32),
            pltpu.VMEM((tokens, width), F32),
            pltpu.VMEM((tokens, width), F32),
            pltpu.VMEM((SLOTS, hidden_units), BF16),
            pltpu.VMEM((SLOTS, hidden_units), BF16),
            pltpu.VMEM((2, 4, *rows), BF16),
            pltpu.VMEM((2, *rows), BF16),
            pltpu.VMEM((2, *rows), BF16),
            pltpu.VMEM((2, *rows), BF16),
            pltpu.VMEM((4, 2, block_rows, width), BF16),
            pltpu.VMEM((2, block_rows, width), BF16),
            pltpu.VMEM((2, block_rows, width), BF16),
            pltpu.VMEM((2, block_rows, width), BF16),
            pltpu.VMEM((2, *rows), BF16),
            pltpu.SemaphoreType.DMA((4,)),
            pltpu.SemaphoreType.DMA((18,)),
            pltpu.SemaphoreType.DMA((18,)),
            pltpu.SemaphoreType.DMA((18,)),
            pltpu.SemaphoreType.DMA((18,)),
            pltpu.SemaphoreType.DMA((16,)),
            pltpu.SemaphoreType.DMA((16,)),
        ],
        compiler_params=pltpu.CompilerParams(
            collective_id=0, has_side_effects=True, vmem_limit_bytes=62 * 2**20
        ),
        name="layer",
    )(
        lengths,
        dec[0],
        q[0],
        k[0],
        v[0],
        gain.reshape(1, width),
        router,
        ids[0],
        win[0],
        wout[0],
        gout[0],
        jnp.asarray(swap_matrix(), BF16),
    )
    return tuple(out[None] for out in outs)


def solution(mesh):
    rows = P("expert", "seq", None)
    return jax.shard_map(
        on_device,
        mesh=mesh,
        in_specs=(rows, rows, rows, rows, P("expert"), P(), P(), rows, rows, rows, rows),
        out_specs=(rows,) * 5,
        check_vma=False,
    )
```

time: 391 us -> 216 us (0.55)
  Pallas kernels: 0 us -> 203 us
  waiting for transfers between devices: 190 us -> 0 us
  blocking collectives: 75.2 us -> 0 us
  matrix products: 45.1 us -> 0 us
  local copies, waits for them, and re-layouts: 33.3 us -> 10.9 us
  starting transfers between devices: 22.3 us -> 0 us
  between operations: 15.3 us -> 1.3 us
  other arithmetic: 8.38 us -> 0 us
    pallas_call x0 -> x1, Pallas kernels: none -> 203 us  [on_device(): pl.pallas_call(layer, out_shape=(shape((tokens, width), BF16), shape((tok...]
    reduce_scatter x3 -> x0, waiting for transfers between devices: 86.6 us -> none  [the longest x2 61.4 us: reduce_rows(): lax.psum_scatter(producer(jnp.int32(0), row_count * lax.axis_size('seq'))...]
    all_gather x4 -> x0, waiting for transfers between devices: 79.8 us -> none  [the longest x2 27 us: gather_rows(): return lax.all_gather(matrix, 'seq', axis=0, tiled=True)]
    all_to_all x2 -> x0, blocking collectives: 75.2 us -> none  [swap_experts(): lax.all_to_all(slot_block, 'expert', split_axis=0, concat_axis=0, tiled=T...]
    dot_general x17 -> x0, matrix products: 41.8 us -> none  [the longest x1 12.1 us: back_project(): jnp.dot(grad_hidden, expert_in[0], preferred_element_type=jnp.float32)]
    all_to_all x2 -> x0, waiting for transfers between devices: 23.1 us -> none  [swap_experts(): lax.all_to_all(slot_block, 'expert', split_axis=0, concat_axis=0, tiled=T...]
    all_to_all x2 -> x0, starting transfers between devices: 21.6 us -> none  [swap_experts(): lax.all_to_all(slot_block, 'expert', split_axis=0, concat_axis=0, tiled=T...]
    reshape x13 -> x0, local copies, waits for them, and re-layouts: 20 us -> none  [the longest x1 2.28 us: on_device(): key_part.reshape(row_count, model_width)]
  transfers between devices with their start and end apart: 9 -> 0, of which waited for: 7 -> 0; matrix products, arithmetic and copies ran while one was open for 12% -> 0% of each run, Pallas kernels for 0% -> 0%
where the time goes in v1:
time: 216 us
  Pallas kernels  203 us (94%)
  local copies, waits for them, and re-layouts  10.9 us (5%)
    pallas_call x1, Pallas kernels, on_device(): pl.pallas_call(layer, out_shape=(shape((tokens, width), BF16), shape((tok...  203 us
    unnamed x9, local copies, waits for them, and re-layouts  10.9 us

profile of v1, /device:TPU:1, one launch (start us, length us, event | category | flops | bytes accessed | tf_op | source)
XLA Modules:
  0.0 215.6 jit_solution(2368900504133760254)
XLA Ops:
  1.3 1.4 copy.17
  2.7 1.7 copy.18.router_ref
  4.4 203.4 %layer.1 = (bf16[128,1024]{1,0:T(8,128)(2,1)}, bf16[128,1024]{1,0:T(8,128)(2,1)}, bf16[128,1024]{1,0:T(8,128)(2,1)}, f32[128,1024]{1,0:T(8,128)}, f32[128,1024]{1,0:T(8,128)}) custom-call(s32[1]{0:T(128)S(6)} %copy.24.length_ref, bf16[128,1024]{1,0:T(8,128)(2,1)} %bitcast.19, bf16[128,1024]{1,0:T(8,128)(2,1)} %bitcast.20, bf16[128,1024]{1,0:T(8,128)(2,1)} %bitcast.21, ...), custom_call_target="tpu_custom_call" | custom-call | tf_op jit(solution)/shard_map/layer/pallas_call | solution.py:476
  207.9 0.0 copy-start
  207.9 1.7 copy.25
  209.6 1.7 copy.26
  211.3 1.7 copy.27
  212.9 1.9 copy.28
  214.8 0.0 copy-done
  214.8 0.8 copy.29
Async XLA Ops:
  207.9 7.0 %copy-start = (f32[128,1024]{1,0:T(8,128)S(1)}, f32[128,1024]{1,0:T(8,128)}, u32[]{:S(2)}) copy-start(f32[128,1024]{1,0:T(8,128)} %get-tuple-element.14) | copy-start | bytes 1572868

commit v2 on v1

--- a/solution.py
+++ b/solution.py
@@ -80,6 +80,10 @@
     knear_l,
     knear_r,
     back_x,
+    slopes,
+    gate_part,
+    gate_near,
+    gate_rows,
     local_sem,
     ag_s,
     ag_r,
@@ -87,6 +91,8 @@
     rs_r,
     xs_s,
     xs_r,
+    gate_s,
+    gate_r,
 ):
     tokens, width = dec_ref.shape
     half = width // 2
@@ -99,6 +105,7 @@
     xc = x * 2 + core
     right = (lax.rem(y + 1, ny), e)
     left = (lax.rem(y + ny - 1, ny), e)
+    across = (lax.rem(y + 2, ny), e)
     hops = (4, 3, 5, 2, 6, 1, 7)
 
     def z_peer(hop):
@@ -122,12 +129,11 @@
         copy.start()
 
     barrier = pltpu.get_barrier_semaphore()
-    for device in (left, right):
+    for device in (left, right, across):
         pl.semaphore_signal(barrier, inc=1, device_id=device, device_id_type=MESH)
     for hop in hops:
         pl.semaphore_signal(barrier, inc=1, device_id=z_peer(hop)[1], device_id_type=MESH)
         pl.semaphore_signal(barrier, inc=1, device_id=xc_peer(hop)[1], device_id_type=MESH)
-    pl.semaphore_wait(barrier, 2 + 2 * len(hops))
 
     class Gather:
         def __init__(self, number, buf, sources):
@@ -152,24 +158,24 @@
                 copy.wait_send()
 
     class Reduce:
-        def __init__(self, number, parts, across, from_left, from_right):
+        def __init__(self, number, parts, crossed, from_left, from_right):
             def at(i):
                 return rs_s.at[number * 6 + i], rs_r.at[number * 6 + i]
 
-            self.parts, self.across = parts, across
+            self.parts, self.crossed = parts, crossed
             self.left_a = remote(parts.at[3, 0], from_right.at[0], *at(0), left)
             self.right_b = remote(parts.at[1, 1], from_left.at[1], *at(1), right)
-            self.opposite_a = remote(parts.at[2, 0], across.at[0], *at(2), right)
-            self.opposite_b = remote(parts.at[2, 1], across.at[1], *at(3), left)
+            self.opposite_a = remote(parts.at[2, 0], crossed.at[0], *at(2), right)
+            self.opposite_b = remote(parts.at[2, 1], crossed.at[1], *at(3), left)
             self.right_a = remote(parts.at[1, 0], from_left.at[0], *at(4), right)
             self.left_b = remote(parts.at[3, 1], from_right.at[1], *at(5), left)
 
         def pass_on(self):
             self.opposite_a.wait_recv()
-            self.parts[1, 0] = (self.parts[1, 0].astype(F32) + self.across[0].astype(F32)).astype(BF16)
+            self.parts[1, 0] = (self.parts[1, 0].astype(F32) + self.crossed[0].astype(F32)).astype(BF16)
             self.right_a.start()
             self.opposite_b.wait_recv()
-            self.parts[3, 1] = (self.parts[3, 1].astype(F32) + self.across[1].astype(F32)).astype(BF16)
+            self.parts[3, 1] = (self.parts[3, 1].astype(F32) + self.crossed[1].astype(F32)).astype(BF16)
             self.left_b.start()
 
         def arrived(self):
@@ -229,17 +235,14 @@
         middle = Dispatch.middle
         sent = Dispatch.sent
 
-    keys = Gather(KV, kvb, (k_ref, v_ref))
-    keys.to_right[0].start()
-    keys.to_left[1].start()
-    keys.to_right[1].start()
-    keys.to_left[0].start()
-
-    ids = ids_ref[...]
-    experts = router_ref.shape[1]
+    experts = router_ref.shape[0]
+    named = [
+        jnp.broadcast_to(ids_ref[j : j + 1, :].astype(F32), (tokens, tokens)).T[:, :experts].astype(jnp.int32)
+        for j in (0, 1)
+    ]
     lanes = lax.broadcasted_iota(jnp.int32, (tokens, experts), 1)
-    first_hot = ids[:, 0:1] == lanes
-    second_hot = ids[:, 1:2] == lanes
+    first_hot = named[0] == lanes
+    second_hot = named[1] == lanes
     ones = first_hot.astype(F32), second_hot.astype(F32)
     earlier = (
         lax.broadcasted_iota(jnp.int32, (tokens, tokens), 0) > lax.broadcasted_iota(jnp.int32, (tokens, tokens), 1)
@@ -259,8 +262,14 @@
     for h in (0, 1):
         send[0, h] = dot_nn(spread, gout_ref[:, h * half : (h + 1) * half]).astype(BF16)
 
+    pl.semaphore_wait(barrier, 3 + 2 * len(hops))
+    keys = Gather(KV, kvb, (k_ref, v_ref))
     grads = Dispatch(AG, 0, gg.at[0])
+    keys.to_right[0].start()
+    keys.to_left[1].start()
     grads.first[0].start()
+    keys.to_right[1].start()
+    keys.to_left[0].start()
     grads.first[1].start()
     keys.forward_right()
     keys.forward_left()
@@ -295,13 +304,12 @@
         residual[:, at] = dec_ref[:, at].astype(F32) + dot_nn(probability.astype(BF16), value_rows)
         return carry
 
-    lax.fori_loop(0, H, attend, 0)
-
     grad_rows = Gather(GR, gg, (gg.at[0, 0], gg.at[0, 1]))
     for h in (0, 1):
         grads.second[h].arrived()
         grad_rows.to_right[h].start()
         grad_rows.to_left[h].start()
+        lax.fori_loop(h * (H // 2), (h + 1) * (H // 2), attend, 0)
 
     whole = residual[...]
     centred = whole - jnp.mean(whole, axis=-1, keepdims=True)
@@ -314,7 +322,7 @@
     rows.first[0].start()
     rows.first[1].start()
 
-    logits = dot_nn(routed_in, router_ref[...])
+    logits = dot_nt(routed_in, router_ref[...])
     first_logit = jnp.sum(jnp.where(first_hot, logits, 0.0), axis=-1, keepdims=True)
     second_logit = jnp.sum(jnp.where(second_hot, logits, 0.0), axis=-1, keepdims=True)
     gates = 1.0 / (1.0 + jnp.exp(second_logit - first_logit)), 1.0 / (1.0 + jnp.exp(first_logit - second_logit))
@@ -351,66 +359,93 @@
             return carry
 
         lax.fori_loop(0, hidden_units // step, up, 0)
+        gate = jnp.zeros((SLOTS, 1), F32)
         for n in range(width // step):
             at = slice(n * step, (n + 1) * step)
             h, low = divmod(n * step, half)
             inner = slice(low, low + step)
             part[0, d, h, :, inner] = dot_nn(ghd[...], win[:, at]).astype(BF16)
-            part[1, d, h, :, inner] = dot_nn(hid[...], wout[:, at]).astype(BF16)
+            result = dot_nn(hid[...], wout[:, at])
+            gate = gate + jnp.sum(result * gg[d, h, :, inner].astype(F32), axis=-1, keepdims=True)
+            part[1, d, h, :, inner] = result.astype(BF16)
+        gate_part[d] = jnp.broadcast_to(gate, (SLOTS, HD)).T[:8]
 
     sums = [Reduce(i, part.at[i], opp.at[i], near_l.at[i], near_r.at[i]) for i in (RG, RO)]
+    gate_sums = [
+        remote(gate_part.at[d], gate_near.at[d - 1], gate_s.at[d - 1], gate_r.at[d - 1], device)
+        for d, device in ((1, right), (2, across), (3, left))
+    ]
     expert(0)
     row_gather.forward_right()
     row_gather.forward_left()
     row_gather.to_right[1].wait_recv()
     expert(3)
-    for total in sums:
-        total.left_a.start()
+    gate_sums[2].start()
+    sums[RG].left_a.start()
     row_gather.to_left[0].wait_recv()
     expert(1)
-    for total in sums:
-        total.right_b.start()
+    gate_sums[0].start()
+    sums[RG].right_b.start()
     grad_rows.on_right.wait_recv()
     grad_rows.on_left.wait_recv()
     row_gather.on_right.wait_recv()
     row_gather.on_left.wait_recv()
     expert(2)
-    for total in sums:
-        total.opposite_a.start()
-        total.opposite_b.start()
-    for total in sums:
-        total.pass_on()
-    returns = []
-    for i in (RG, RO):
-        sums[i].arrived()
+    gate_sums[1].start()
+    sums[RG].opposite_a.start()
+    sums[RG].opposite_b.start()
+    sums[RG].pass_on()
+    for copy in (sums[RO].opposite_a, sums[RO].opposite_b, sums[RO].right_b, sums[RO].left_a):
+        copy.start()
+
+    for copy in gate_sums:
+        copy.wait_recv()
+    gate_total = gate_part[0] + gate_near[0] + gate_near[1] + gate_near[2]
+    rest = jnp.broadcast_to(gate_total[0:1], (HD, SLOTS)).T
+    piece_lanes = lax.broadcasted_iota(jnp.int32, (SLOTS, HD), 1)
+    packed = jnp.zeros((SLOTS, HD), F32)
+    for n in range(3):
+        piece = rest.astype(BF16).astype(F32)
+        packed = packed + jnp.where(piece_lanes == n, piece, 0.0)
+        rest = rest - piece
+    gate_rows[0] = packed.astype(BF16)
+    gate_first = Stage(16, gate_rows.at[0], gate_rows.at[1], xc_peer, xc)
+    gate_second = Stage(17, gate_rows.at[2], gate_rows.at[3], z_peer, z)
+    gate_first.start()
+
+    def send_back(i):
         back = Return((BG, BO)[i], 2 + i, back_x.at[i])
         for h in (0, 1):
             send[2 + i, h] = (
                 part[i, 0, h].astype(F32) + near_l[i, h].astype(F32) + near_r[i, h].astype(F32)
             ).astype(BF16)
             back.first[h].start()
-        returns.append(back)
-    for back in returns:
-        back.middle(0)
-        back.middle(1)
-    for back in returns:
-        back.second[0].arrived()
-        back.second[1].arrived()
-
-    outs, grad_routed = [], None
+        return back
+
+    sums[RG].arrived()
+    grads_back = send_back(RG)
+    gate_first.arrived()
+    turn(gate_rows.at[1], gate_rows.at[2])
+    gate_second.start()
+    grads_back.middle(0)
+    grads_back.middle(1)
+    sums[RO].pass_on()
+    gate_second.arrived()
+    grads_back.second[0].arrived()
+    grads_back.second[1].arrived()
+
+    cotangent = gout_ref[...].astype(F32)
+    grad_routed, gate_grads = None, []
     for j in (0, 1):
-        outs.append(jnp.concatenate([dot_nn(pick[j], back_x[1, h]) for h in (0, 1)], axis=1))
-        grad = gates[j] * jnp.concatenate([dot_nn(pick[j], back_x[0, h]) for h in (0, 1)], axis=1)
+        grad = gates[j] * jnp.concatenate([dot_nn(pick[j], back_x[RG, h]) for h in (0, 1)], axis=1)
         grad_routed = grad if grad_routed is None else grad_routed + grad
-    layer_ref[...] = (residual[...] + gates[0] * outs[0] + gates[1] * outs[1]).astype(BF16)
-    cotangent = gout_ref[...].astype(F32)
-    gate_grads = [jnp.sum(cotangent * out, axis=-1, keepdims=True) for out in outs]
+        gate_grads.append(jnp.sum(dot_nn(pick[j], gate_rows[3]), axis=-1, keepdims=True))
     gate_mean = gates[0] * gate_grads[0] + gates[1] * gate_grads[1]
     parts = [gates[j] * (gate_grads[j] - gate_mean) for j in (0, 1)]
     rest = jnp.where(first_hot, parts[0], 0.0) + jnp.where(second_hot, parts[1], 0.0)
     for _ in range(3):
         piece = rest.astype(BF16)
-        grad_routed = grad_routed + dot_nt(piece, router_ref[...])
+        grad_routed = grad_routed + dot_nn(piece, router_ref[...])
         rest = rest - piece.astype(F32)
     grad_norm = grad_routed * gain_ref[...]
     state = normed[...]
@@ -421,29 +456,47 @@
     )
     gstates_ref[...] = grad_states.astype(BF16)
 
-    def attend_back(head, carry):
+    def value_grads(head, carry):
+        at = columns(head)
+        rows_of = dot_tn(prob[head].astype(BF16), gstates_ref[:, at]).astype(BF16)
+        kpart[:, 1, :, at] = rows_of.reshape(ny, block_rows, HD)
+        return carry
+
+    def key_grads(head, carry):
+        at = columns(head)
+        value_rows = kvb[:, 1, :, at].reshape(sources, HD)
+        probability = prob[head]
+        grad_probability = dot_nt(gstates_ref[:, at], value_rows)
+        inner = jnp.sum(probability * grad_probability, axis=-1, keepdims=True)
+        grad_scores = (probability * (grad_probability - inner)).astype(BF16)
+        slopes[head] = grad_scores
+        rows_of = (dot_tn(grad_scores, q_ref[:, at]) * score_scale).astype(BF16)
+        kpart[:, 0, :, at] = rows_of.reshape(ny, block_rows, HD)
+        return carry
+
+    def query_grads(head, carry):
         at = columns(head)
         key_rows = kvb[:, 0, :, at].reshape(sources, HD)
-        value_rows = kvb[:, 1, :, at].reshape(sources, HD)
-        probability = prob[head]
-        grad_head = gstates_ref[:, at]
-        grad_probability = dot_nt(grad_head, value_rows)
-        inner = jnp.sum(probability * grad_probability, axis=-1, keepdims=True)
-        grad_scores = (probability * (grad_probability - inner)).astype(BF16)
-        gq_ref[:, at] = (dot_nn(grad_scores, key_rows) * score_scale).astype(BF16)
-        key_part = (dot_tn(grad_scores, q_ref[:, at]) * score_scale).astype(BF16)
-        value_part = dot_tn(probability.astype(BF16), grad_head).astype(BF16)
-        kpart[:, 0, :, at] = key_part.reshape(ny, block_rows, HD)
-        kpart[:, 1, :, at] = value_part.reshape(ny, block_rows, HD)
+        gq_ref[:, at] = (dot_nn(slopes[head], key_rows) * score_scale).astype(BF16)
         return carry
 
-    lax.fori_loop(0, H, attend_back, 0)
     key_sum = Reduce(RKV, kpart, kopp, knear_l, knear_r)
-    key_sum.opposite_a.start()
+    lax.fori_loop(0, H, value_grads, 0)
     key_sum.opposite_b.start()
     key_sum.right_b.start()
+    lax.fori_loop(0, H, key_grads, 0)
+    key_sum.opposite_a.start()
     key_sum.left_a.start()
+    sums[RO].arrived()
+    outs_back = send_back(RO)
+    lax.fori_loop(0, H, query_grads, 0)
+    outs_back.middle(0)
+    outs_back.middle(1)
     key_sum.pass_on()
+    outs_back.second[0].arrived()
+    outs_back.second[1].arrived()
+    outs = [jnp.concatenate([dot_nn(pick[j], back_x[RO, h]) for h in (0, 1)], axis=1) for j in (0, 1)]
+    layer_ref[...] = (residual[...] + gates[0] * outs[0] + gates[1] * outs[1]).astype(BF16)
     key_sum.arrived()
     for h, out in ((0, gk_ref), (1, gv_ref)):
         out[...] = kpart[0, h].astype(F32) + knear_l[h].astype(F32) + knear_r[h].astype(F32)
@@ -452,8 +505,20 @@
         gather.sent()
     for total in (*sums, key_sum):
         total.sent()
-    for exchange in (grads, rows, *returns):
+    for exchange in (grads, rows, grads_back, outs_back, gate_first, gate_second):
         exchange.sent()
+    for copy in gate_sums:
+        copy.wait_send()
+
+
+def hand_over(*refs):
+    *refs, sems = refs
+    count = len(refs) // 2
+    copies = [pltpu.make_async_copy(refs[i], refs[count + i], sems.at[i]) for i in range(count)]
+    for copy in copies:
+        copy.start()
+    for copy in copies:
+        copy.wait()
 
 
 def swap_matrix():
@@ -521,13 +586,19 @@
             pltpu.VMEM((2, block_rows, width), BF16),
             pltpu.VMEM((2, block_rows, width), BF16),
             pltpu.VMEM((2, *rows), BF16),
+            pltpu.VMEM((H, tokens, 4 * block_rows), BF16),
+            pltpu.VMEM((4, 8, SLOTS), F32),
+            pltpu.VMEM((3, 8, SLOTS), F32),
+            pltpu.VMEM((4, SLOTS, HD), BF16),
             pltpu.SemaphoreType.DMA((4,)),
             pltpu.SemaphoreType.DMA((18,)),
             pltpu.SemaphoreType.DMA((18,)),
             pltpu.SemaphoreType.DMA((18,)),
             pltpu.SemaphoreType.DMA((18,)),
-            pltpu.SemaphoreType.DMA((16,)),
-            pltpu.SemaphoreType.DMA((16,)),
+            pltpu.SemaphoreType.DMA((18,)),
+            pltpu.SemaphoreType.DMA((18,)),
+            pltpu.SemaphoreType.DMA((3,)),
+            pltpu.SemaphoreType.DMA((3,)),
         ],
         compiler_params=pltpu.CompilerParams(
             collective_id=0, has_side_effects=True, vmem_limit_bytes=62 * 2**20
@@ -540,13 +611,22 @@
         k[0],
         v[0],
         gain.reshape(1, width),
-        router,
-        ids[0],
+        router.T,
+        ids[0].T,
         win[0],
         wout[0],
         gout[0],
         jnp.asarray(swap_matrix(), BF16),
     )
+    count = len(outs)
+    outs = pl.pallas_call(
+        hand_over,
+        out_shape=tuple(shape(out.shape, out.dtype) for out in outs),
+        in_specs=[hbm] * count,
+        out_specs=[hbm] * count,
+        scratch_shapes=[pltpu.SemaphoreType.DMA((count,))],
+        name="hand_over",
+    )(*outs)
     return tuple(out[None] for out in outs)
 
 

time: 216 us -> 239 us (1.11)
  Pallas kernels: 203 us -> 237 us
  local copies, waits for them, and re-layouts: 10.9 us -> 0 us
    pallas_call x0 -> x1, Pallas kernels: none -> 56.7 us  [on_device(): pl.pallas_call(hand_over, out_shape=tuple((shape(out.shape, out.dtype) fo...]
    pallas_call x1, Pallas kernels: 203 us -> 181 us  [on_device(): pl.pallas_call(layer, out_shape=(shape((tokens, width), BF16), shape((tok...]
    unnamed x9 -> x0, local copies, waits for them, and re-layouts: 10.9 us -> none
where the time goes in v2:
time: 239 us
  Pallas kernels  237 us (99%)
    pallas_call x1, Pallas kernels, on_device(): pl.pallas_call(layer, out_shape=(shape((tokens, width), BF16), shape((tok...  181 us
    pallas_call x1, Pallas kernels, on_device(): pl.pallas_call(hand_over, out_shape=tuple((shape(out.shape, out.dtype) fo...  56.7 us

profile of v2, /device:TPU:1, one launch (start us, length us, event | category | flops | bytes accessed | tf_op | source)
XLA Modules:
  0.0 238.8 jit_solution(4891060974672818768)
XLA Ops:
  1.3 180.6 %layer.1 = (bf16[128,1024]{1,0:T(8,128)(2,1)}, bf16[128,1024]{1,0:T(8,128)(2,1)}, bf16[128,1024]{1,0:T(8,128)(2,1)}, f32[128,1024]{1,0:T(8,128)}, f32[128,1024]{1,0:T(8,128)}) custom-call(s32[1]{0:T(128)S(6)} %copy.17.length_ref, bf16[128,1024]{1,0:T(8,128)(2,1)} %bitcast.19, bf16[128,1024]{1,0:T(8,128)(2,1)} %bitcast.20, bf16[128,1024]{1,0:T(8,128)(2,1)} %bitcast.21, ...), custom_call_target="tpu_custom_call" | custom-call | tf_op jit(solution)/shard_map/layer/pallas_call | solution.py:541
  181.9 56.7 %hand_over.1 = (bf16[128,1024]{1,0:T(8,128)(2,1)}, bf16[128,1024]{1,0:T(8,128)(2,1)}, bf16[128,1024]{1,0:T(8,128)(2,1)}, f32[128,1024]{1,0:T(8,128)}, f32[128,1024]{1,0:T(8,128)}) custom-call(bf16[128,1024]{1,0:T(8,128)(2,1)} %get-tuple-element.15.refs_0_, bf16[128,1024]{1,0:T(8,128)(2,1)} %get-tuple-element.16.refs_1_, ...), custom_call_target="tpu_custom_call" | custom-call | tf_op jit(solution)/shard_map/hand_over/pallas_call | solution.py:622

commit v3 on v2

--- a/solution.py
+++ b/solution.py
@@ -84,6 +84,8 @@
     gate_part,
     gate_near,
     gate_rows,
+    landed,
+    ready,
     local_sem,
     ag_s,
     ag_r,
@@ -170,13 +172,19 @@
             self.right_a = remote(parts.at[1, 0], from_left.at[0], *at(4), right)
             self.left_b = remote(parts.at[3, 1], from_right.at[1], *at(5), left)
 
-        def pass_on(self):
+        def pass_a(self):
             self.opposite_a.wait_recv()
             self.parts[1, 0] = (self.parts[1, 0].astype(F32) + self.crossed[0].astype(F32)).astype(BF16)
             self.right_a.start()
+
+        def pass_b(self):
             self.opposite_b.wait_recv()
             self.parts[3, 1] = (self.parts[3, 1].astype(F32) + self.crossed[1].astype(F32)).astype(BF16)
             self.left_b.start()
+
+        def pass_on(self):
+            self.pass_a()
+            self.pass_b()
 
         def arrived(self):
             for copy in (self.left_a, self.right_b, self.right_a, self.left_b):
@@ -211,29 +219,32 @@
     def turn(src, dst):
         dst[...] = dot_nn(swap_ref[...], src[...]).astype(BF16)
 
-    class Dispatch:
-        def __init__(self, number, tensor, dst):
-            self.first = [Stage(number * 4 + h, send.at[tensor, h], zbuf.at[tensor, h], z_peer, z) for h in (0, 1)]
-            self.second = [Stage(number * 4 + 2 + h, turned.at[tensor, h], dst.at[h], xc_peer, xc) for h in (0, 1)]
-            self.tensor = tensor
+    class Exchange:
+        def __init__(self, number, tensor, dst, stages):
+            here = (send, zbuf, turned)
+            self.first, self.second, self.tensor, self.dst = [], [], tensor, dst
+            for h in (0, 1):
+                leave, between, go_on = (buf.at[tensor, h] for buf in here)
+                end = dst.at[0] if h == 0 else landed.at[tensor]
+                one, two = stages if h == 0 else stages[::-1]
+                self.first.append(Stage(number * 4 + h, leave, between, *one))
+                self.second.append(Stage(number * 4 + 2 + h, go_on, end, *two))
 
         def middle(self, h):
             self.first[h].arrived()
             turn(zbuf.at[self.tensor, h], turned.at[self.tensor, h])
             self.second[h].start()
 
+        def finish(self, h):
+            self.second[h].arrived()
+            if h == 1:
+                turn(landed.at[self.tensor], self.dst.at[1])
+
         def sent(self):
             for stage in (*self.first, *self.second):
                 stage.sent()
 
-    class Return:
-        def __init__(self, number, tensor, dst):
-            self.first = [Stage(number * 4 + h, send.at[tensor, h], zbuf.at[tensor, h], xc_peer, xc) for h in (0, 1)]
-            self.second = [Stage(number * 4 + 2 + h, turned.at[tensor, h], dst.at[h], z_peer, z) for h in (0, 1)]
-            self.tensor = tensor
-
-        middle = Dispatch.middle
-        sent = Dispatch.sent
+    along_z, along_xc = (z_peer, z), (xc_peer, xc)
 
     experts = router_ref.shape[0]
     named = [
@@ -258,13 +269,14 @@
         chosen = (slot.astype(jnp.int32) == slot_lanes).astype(F32)
         pick[j] = chosen.astype(BF16)
         both = both + chosen
-    spread = both.T.astype(BF16)
+    spread = [both.T.astype(BF16)]
+    spread.append(dot_nn(swap_ref[...], spread[0]).astype(BF16))
     for h in (0, 1):
-        send[0, h] = dot_nn(spread, gout_ref[:, h * half : (h + 1) * half]).astype(BF16)
+        send[0, h] = dot_nn(spread[h], gout_ref[:, h * half : (h + 1) * half]).astype(BF16)
 
     pl.semaphore_wait(barrier, 3 + 2 * len(hops))
     keys = Gather(KV, kvb, (k_ref, v_ref))
-    grads = Dispatch(AG, 0, gg.at[0])
+    grads = Exchange(AG, 0, gg.at[0], (along_z, along_xc))
     keys.to_right[0].start()
     keys.to_left[1].start()
     grads.first[0].start()
@@ -273,8 +285,8 @@
     grads.first[1].start()
     keys.forward_right()
     keys.forward_left()
+    grads.middle(1)
     grads.middle(0)
-    grads.middle(1)
     keys.to_right[1].wait_recv()
     keys.to_left[0].wait_recv()
     own_k.wait()
@@ -306,7 +318,7 @@
 
     grad_rows = Gather(GR, gg, (gg.at[0, 0], gg.at[0, 1]))
     for h in (0, 1):
-        grads.second[h].arrived()
+        grads.finish(h)
         grad_rows.to_right[h].start()
         grad_rows.to_left[h].start()
         lax.fori_loop(h * (H // 2), (h + 1) * (H // 2), attend, 0)
@@ -317,8 +329,8 @@
     normed[...] = centred * reciprocal
     routed_in = (normed[...] * gain_ref[...]).astype(BF16)
     for h in (0, 1):
-        send[1, h] = dot_nn(spread, routed_in[:, h * half : (h + 1) * half]).astype(BF16)
-    rows = Dispatch(AX, 1, xg.at[0])
+        send[1, h] = dot_nn(spread[h], routed_in[:, h * half : (h + 1) * half]).astype(BF16)
+    rows = Exchange(AX, 1, xg.at[0], (along_z, along_xc))
     rows.first[0].start()
     rows.first[1].start()
 
@@ -327,35 +339,29 @@
     second_logit = jnp.sum(jnp.where(second_hot, logits, 0.0), axis=-1, keepdims=True)
     gates = 1.0 / (1.0 + jnp.exp(second_logit - first_logit)), 1.0 / (1.0 + jnp.exp(first_logit - second_logit))
 
-    grad_rows.forward_right()
-    rows.middle(0)
-    grad_rows.forward_left()
-    rows.middle(1)
-    row_gather = Gather(XR, xg, (xg.at[0, 0], xg.at[0, 1]))
-    for h in (0, 1):
-        rows.second[h].arrived()
-        row_gather.to_right[h].start()
-        row_gather.to_left[h].start()
-    own_in.wait()
-    own_out.wait()
-    grad_rows.to_right[1].wait_recv()
-    grad_rows.to_left[0].wait_recv()
-
     hidden_units = win.shape[0]
     step = 256
+
+    def prepare(d):
+        def up(i, carry):
+            at = pl.ds(pl.multiple_of(i * step, step), step)
+            weight_out = wout[at, :]
+            ready[d, :, at] = dot_nt(gg[d, 0], weight_out[:, :half]) + dot_nt(gg[d, 1], weight_out[:, half:])
+            return carry
+
+        lax.fori_loop(0, hidden_units // step, up, 0)
 
     def expert(d):
         def up(i, carry):
             at = pl.ds(pl.multiple_of(i * step, step), step)
-            weight_in, weight_out = win[at, :], wout[at, :]
+            weight_in = win[at, :]
             signal = dot_nt(xg[d, 0], weight_in[:, :half]) + dot_nt(xg[d, 1], weight_in[:, half:])
-            cotangent = dot_nt(gg[d, 0], weight_out[:, :half]) + dot_nt(gg[d, 1], weight_out[:, half:])
             square = signal * signal
             tangent = jnp.tanh(gelu_scale * (signal + cubic_weight * signal * square))
             upper = 0.5 * (1.0 + tangent)
             hid[:, at] = (signal * upper).astype(BF16)
             slope = upper + 0.5 * signal * (1.0 - tangent * tangent) * gelu_scale * (1.0 + 3.0 * cubic_weight * square)
-            ghd[:, at] = (cotangent * slope).astype(BF16)
+            ghd[:, at] = (ready[d, :, at] * slope).astype(BF16)
             return carry
 
         lax.fori_loop(0, hidden_units // step, up, 0)
@@ -375,9 +381,29 @@
         remote(gate_part.at[d], gate_near.at[d - 1], gate_s.at[d - 1], gate_r.at[d - 1], device)
         for d, device in ((1, right), (2, across), (3, left))
     ]
+    row_gather = Gather(XR, xg, (xg.at[0, 0], xg.at[0, 1]))
+    grad_rows.forward_right()
+    own_out.wait()
+    prepare(0)
+    rows.middle(1)
+    rows.middle(0)
+    grad_rows.forward_left()
+    for h in (0, 1):
+        rows.finish(h)
+        row_gather.to_right[h].start()
+        row_gather.to_left[h].start()
+    grad_rows.to_right[1].wait_recv()
+    prepare(3)
+    grad_rows.to_left[0].wait_recv()
+    prepare(1)
+    own_in.wait()
+
     expert(0)
     row_gather.forward_right()
     row_gather.forward_left()
+    grad_rows.on_right.wait_recv()
+    grad_rows.on_left.wait_recv()
+    prepare(2)
     row_gather.to_right[1].wait_recv()
     expert(3)
     gate_sums[2].start()
@@ -386,8 +412,6 @@
     expert(1)
     gate_sums[0].start()
     sums[RG].right_b.start()
-    grad_rows.on_right.wait_recv()
-    grad_rows.on_left.wait_recv()
     row_gather.on_right.wait_recv()
     row_gather.on_left.wait_recv()
     expert(2)
@@ -414,11 +438,11 @@
     gate_first.start()
 
     def send_back(i):
-        back = Return((BG, BO)[i], 2 + i, back_x.at[i])
+        back = Exchange((BG, BO)[i], 2 + i, back_x.at[i], (along_xc, along_z))
         for h in (0, 1):
-            send[2 + i, h] = (
-                part[i, 0, h].astype(F32) + near_l[i, h].astype(F32) + near_r[i, h].astype(F32)
-            ).astype(BF16)
+            total = part[i, 0, h].astype(F32) + near_l[i, h].astype(F32) + near_r[i, h].astype(F32)
+            total = total.astype(BF16)
+            send[2 + i, h] = total if h == 0 else dot_nn(swap_ref[...], total).astype(BF16)
             back.first[h].start()
         return back
 
@@ -431,8 +455,8 @@
     grads_back.middle(1)
     sums[RO].pass_on()
     gate_second.arrived()
-    grads_back.second[0].arrived()
-    grads_back.second[1].arrived()
+    grads_back.finish(0)
+    grads_back.finish(1)
 
     cotangent = gout_ref[...].astype(F32)
     grad_routed, gate_grads = None, []
@@ -484,17 +508,18 @@
     lax.fori_loop(0, H, value_grads, 0)
     key_sum.opposite_b.start()
     key_sum.right_b.start()
+    sums[RO].arrived()
+    outs_back = send_back(RO)
     lax.fori_loop(0, H, key_grads, 0)
     key_sum.opposite_a.start()
     key_sum.left_a.start()
-    sums[RO].arrived()
-    outs_back = send_back(RO)
+    outs_back.middle(0)
+    key_sum.pass_b()
+    outs_back.middle(1)
     lax.fori_loop(0, H, query_grads, 0)
-    outs_back.middle(0)
-    outs_back.middle(1)
-    key_sum.pass_on()
-    outs_back.second[0].arrived()
-    outs_back.second[1].arrived()
+    key_sum.pass_a()
+    outs_back.finish(0)
+    outs_back.finish(1)
     outs = [jnp.concatenate([dot_nn(pick[j], back_x[RO, h]) for h in (0, 1)], axis=1) for j in (0, 1)]
     layer_ref[...] = (residual[...] + gates[0] * outs[0] + gates[1] * outs[1]).astype(BF16)
     key_sum.arrived()
@@ -512,13 +537,9 @@
 
 
 def hand_over(*refs):
-    *refs, sems = refs
     count = len(refs) // 2
-    copies = [pltpu.make_async_copy(refs[i], refs[count + i], sems.at[i]) for i in range(count)]
-    for copy in copies:
-        copy.start()
-    for copy in copies:
-        copy.wait()
+    for source, target in zip(refs[:count], refs[count:]):
+        target[...] = source[...]
 
 
 def swap_matrix():
@@ -590,6 +611,8 @@
             pltpu.VMEM((4, 8, SLOTS), F32),
             pltpu.VMEM((3, 8, SLOTS), F32),
             pltpu.VMEM((4, SLOTS, HD), BF16),
+            pltpu.VMEM((4, SLOTS, half), BF16),
+            pltpu.VMEM((4, SLOTS, hidden_units), F32),
             pltpu.SemaphoreType.DMA((4,)),
             pltpu.SemaphoreType.DMA((18,)),
             pltpu.SemaphoreType.DMA((18,)),
@@ -622,9 +645,9 @@
     outs = pl.pallas_call(
         hand_over,
         out_shape=tuple(shape(out.shape, out.dtype) for out in outs),
-        in_specs=[hbm] * count,
-        out_specs=[hbm] * count,
-        scratch_shapes=[pltpu.SemaphoreType.DMA((count,))],
+        grid=(2,),
+        in_specs=[pl.BlockSpec((out.shape[0] // 2, width), lambda i: (i, 0)) for out in outs],
+        out_specs=[pl.BlockSpec((out.shape[0] // 2, width), lambda i: (i, 0)) for out in outs],
         name="hand_over",
     )(*outs)
     return tuple(out[None] for out in outs)

time: 239 us -> 167 us (0.70)
  Pallas kernels: 237 us -> 166 us
    pallas_call x1, Pallas kernels: 56.7 us -> 2.51 us  [on_device(): pl.pallas_call(hand_over, out_shape=tuple((shape(out.shape, out.dtype) fo...]
    pallas_call x1, Pallas kernels: 181 us -> 163 us  [on_device(): pl.pallas_call(layer, out_shape=(shape((tokens, width), BF16), shape((tok...]
where the time goes in v3:
time: 167 us
  Pallas kernels  166 us (99%)
    pallas_call x1, Pallas kernels, on_device(): pl.pallas_call(layer, out_shape=(shape((tokens, width), BF16), shape((tok...  163 us

profile of v3, /device:TPU:1, one launch (start us, length us, event | category | flops | bytes accessed | tf_op | source)
XLA Modules:
  0.0 166.9 jit_solution(11376236763576105771)
XLA Ops:
  1.3 163.0 %layer.1 = (bf16[128,1024]{1,0:T(8,128)(2,1)}, bf16[128,1024]{1,0:T(8,128)(2,1)}, bf16[128,1024]{1,0:T(8,128)(2,1)}, f32[128,1024]{1,0:T(8,128)}, f32[128,1024]{1,0:T(8,128)}) custom-call(s32[1]{0:T(128)S(6)} %copy.17.length_ref, bf16[128,1024]{1,0:T(8,128)(2,1)} %bitcast.19, bf16[128,1024]{1,0:T(8,128)(2,1)} %bitcast.20, bf16[128,1024]{1,0:T(8,128)(2,1)} %bitcast.21, ...), custom_call_target="tpu_custom_call" | custom-call | tf_op jit(solution)/shard_map/layer/pallas_call | solution.py:562
  164.3 2.5 %hand_over.1 = (bf16[128,1024]{1,0:T(8,128)(2,1)}, bf16[128,1024]{1,0:T(8,128)(2,1)}, bf16[128,1024]{1,0:T(8,128)(2,1)}, f32[128,1024]{1,0:T(8,128)}, f32[128,1024]{1,0:T(8,128)}) custom-call(bf16[128,1024]{1,0:T(8,128)(2,1)} %get-tuple-element.15.refs_0_, bf16[128,1024]{1,0:T(8,128)(2,1)} %get-tuple-element.16.refs_1_, ...), custom_call_target="tpu_custom_call" | custom-call | tf_op jit(solution)/shard_map/hand_over/pallas_call | solution.py:645

commit v4 on v3

--- a/solution.py
+++ b/solution.py
@@ -23,7 +23,7 @@
 cubic_weight = 0.044715
 
 KV, GR, XR = 0, 1, 2
-RG, RO, RKV = 0, 1, 2
+RG, RO, RKV, RT = 0, 1, 2, 3
 AG, AX, BG, BO = 0, 1, 2, 3
 
 
@@ -75,6 +75,18 @@
     opp,
     near_l,
     near_r,
+    gpart,
+    gopp,
+    gnear_l,
+    gnear_r,
+    wide,
+    far,
+    tpart,
+    topp,
+    tnear_l,
+    tnear_r,
+    note,
+    note_near,
     kpart,
     kopp,
     knear_l,
@@ -95,6 +107,8 @@
     xs_r,
     gate_s,
     gate_r,
+    note_s,
+    note_r,
 ):
     tokens, width = dec_ref.shape
     half = width // 2
@@ -247,34 +261,45 @@
     along_z, along_xc = (z_peer, z), (xc_peer, xc)
 
     experts = router_ref.shape[0]
-    named = [
-        jnp.broadcast_to(ids_ref[j : j + 1, :].astype(F32), (tokens, tokens)).T[:, :experts].astype(jnp.int32)
-        for j in (0, 1)
-    ]
     lanes = lax.broadcasted_iota(jnp.int32, (tokens, experts), 1)
-    first_hot = named[0] == lanes
-    second_hot = named[1] == lanes
-    ones = first_hot.astype(F32), second_hot.astype(F32)
     earlier = (
         lax.broadcasted_iota(jnp.int32, (tokens, tokens), 0) > lax.broadcasted_iota(jnp.int32, (tokens, tokens), 1)
     ).astype(F32).astype(BF16)
     slot_lanes = lax.broadcasted_iota(jnp.int32, (tokens, SLOTS), 1)
     base = ((lanes // 2) % SIDE) * GROUP + (lanes // (2 * SIDE)) * (2 * CAP) + (lanes % 2) * CAP
-    both = jnp.zeros((tokens, SLOTS), F32)
-    for j in (0, 1):
-        rank = dot_nn(earlier, ones[j].astype(BF16))
-        if j == 1:
-            rank = rank + jnp.sum(ones[0], axis=0, keepdims=True)
-        slot = jnp.sum(ones[j] * (rank + base.astype(F32)), axis=-1, keepdims=True)
-        chosen = (slot.astype(jnp.int32) == slot_lanes).astype(F32)
-        pick[j] = chosen.astype(BF16)
-        both = both + chosen
+
+    def upright(row):
+        return jnp.broadcast_to(row, (tokens, tokens)).T
+
+    def choose(d, names):
+        hot = [upright(names[j : j + 1]).astype(jnp.int32)[:, :experts] == lanes for j in (0, 1)]
+        ones = [h.astype(F32) for h in hot]
+        both = jnp.zeros((tokens, SLOTS), F32)
+        for j in (0, 1):
+            rank = dot_nn(earlier, ones[j].astype(BF16))
+            if j == 1:
+                rank = rank + jnp.sum(ones[0], axis=0, keepdims=True)
+            slot = jnp.sum(ones[j] * (rank + base.astype(F32)), axis=-1, keepdims=True)
+            chosen = (slot.astype(jnp.int32) == slot_lanes).astype(F32)
+            pick[d, j] = chosen.astype(BF16)
+            both = both + chosen
+        return hot, both
+
+    sublanes = lax.broadcasted_iota(jnp.int32, (8, tokens), 0)
+    ids = [jnp.broadcast_to(ids_ref[j : j + 1, :].astype(F32), (8, tokens)) for j in (0, 1)]
+    note[0] = jnp.where(sublanes == 0, ids[0], ids[1])
+    (first_hot, second_hot), both = choose(0, note[0])
     spread = [both.T.astype(BF16)]
     spread.append(dot_nn(swap_ref[...], spread[0]).astype(BF16))
     for h in (0, 1):
         send[0, h] = dot_nn(spread[h], gout_ref[:, h * half : (h + 1) * half]).astype(BF16)
 
     pl.semaphore_wait(barrier, 3 + 2 * len(hops))
+    notes = [
+        remote(note.at[n], note_near.at[n, d - 1], note_s.at[n * 3 + d - 1], note_r.at[n * 3 + d - 1], device)
+        for n in (0, 1)
+        for d, device in ((1, left), (2, across), (3, right))
+    ]
     keys = Gather(KV, kvb, (k_ref, v_ref))
     grads = Exchange(AG, 0, gg.at[0], (along_z, along_xc))
     keys.to_right[0].start()
@@ -283,6 +308,8 @@
     keys.to_right[1].start()
     keys.to_left[0].start()
     grads.first[1].start()
+    for copy in notes[:3]:
+        copy.start()
     keys.forward_right()
     keys.forward_left()
     grads.middle(1)
@@ -370,19 +397,34 @@
             at = slice(n * step, (n + 1) * step)
             h, low = divmod(n * step, half)
             inner = slice(low, low + step)
-            part[0, d, h, :, inner] = dot_nn(ghd[...], win[:, at]).astype(BF16)
+            grad = dot_nn(ghd[...], win[:, at]).astype(BF16)
+            if h == 0:
+                gpart[d, n] = grad
+            else:
+                wide[d, :, inner] = grad
             result = dot_nn(hid[...], wout[:, at])
             gate = gate + jnp.sum(result * gg[d, h, :, inner].astype(F32), axis=-1, keepdims=True)
-            part[1, d, h, :, inner] = result.astype(BF16)
+            part[d, h, :, inner] = result.astype(BF16)
         gate_part[d] = jnp.broadcast_to(gate, (SLOTS, HD)).T[:8]
 
-    sums = [Reduce(i, part.at[i], opp.at[i], near_l.at[i], near_r.at[i]) for i in (RG, RO)]
+    sums = [
+        Reduce(RG, gpart, gopp, gnear_l, gnear_r),
+        Reduce(RO, part, opp, near_l, near_r),
+    ]
+    token_sum = Reduce(RT, tpart, topp, tnear_l, tnear_r)
     gate_sums = [
         remote(gate_part.at[d], gate_near.at[d - 1], gate_s.at[d - 1], gate_r.at[d - 1], device)
         for d, device in ((1, right), (2, across), (3, left))
     ]
+    tall = [jnp.broadcast_to(gate, (tokens, tokens)).T[:8] for gate in gates]
+    note[1] = jnp.where(sublanes == 0, tall[0], tall[1])
+    for copy in notes[3:]:
+        copy.start()
     row_gather = Gather(XR, xg, (xg.at[0, 0], xg.at[0, 1]))
     grad_rows.forward_right()
+    for d in (1, 2, 3):
+        notes[d - 1].wait_recv()
+        choose(d, note_near[0, d - 1])
     own_out.wait()
     prepare(0)
     rows.middle(1)
@@ -398,7 +440,29 @@
     prepare(1)
     own_in.wait()
 
+    halfway = [zbuf.at[2, 1], *(far.at[0, d] for d in range(3))]
+    onward = [turned.at[2, 1], *(far.at[1, d] for d in range(3))]
+    home = [landed.at[2], *(far.at[2, d] for d in range(3))]
+    wide_first = [Stage(18 + 2 * d, wide.at[d], halfway[d], xc_peer, xc) for d in range(4)]
+    wide_second = [Stage(19 + 2 * d, onward[d], home[d], z_peer, z) for d in range(4)]
+
+    def go_on(d):
+        wide_first[d].arrived()
+        turn(halfway[d], onward[d])
+        wide_second[d].start()
+
+    def to_tokens(d):
+        wide_second[d].arrived()
+        rows_home = home[d][...]
+        total = jnp.zeros((tokens, half), F32)
+        for j in (0, 1):
+            gate = gates[j] if d == 0 else upright(note_near[1, d - 1][j : j + 1])[:, 0:1]
+            total = total + gate * dot_nn(pick[d, j], rows_home)
+        for h in (0, 1):
+            tpart[d, h] = total[:, h * (half // 2) : (h + 1) * (half // 2)].astype(BF16)
+
     expert(0)
+    wide_first[0].start()
     row_gather.forward_right()
     row_gather.forward_left()
     grad_rows.on_right.wait_recv()
@@ -408,19 +472,31 @@
     expert(3)
     gate_sums[2].start()
     sums[RG].left_a.start()
+    wide_first[3].start()
+    sums[RO].left_a.start()
+    go_on(0)
     row_gather.to_left[0].wait_recv()
     expert(1)
     gate_sums[0].start()
     sums[RG].right_b.start()
+    wide_first[1].start()
+    sums[RO].right_b.start()
+    go_on(3)
     row_gather.on_right.wait_recv()
     row_gather.on_left.wait_recv()
     expert(2)
     gate_sums[1].start()
     sums[RG].opposite_a.start()
     sums[RG].opposite_b.start()
+    wide_first[2].start()
+    sums[RO].opposite_a.start()
+    sums[RO].opposite_b.start()
+    go_on(1)
+    for copy in notes[3:]:
+        copy.wait_recv()
+    to_tokens(0)
+    go_on(2)
     sums[RG].pass_on()
-    for copy in (sums[RO].opposite_a, sums[RO].opposite_b, sums[RO].right_b, sums[RO].left_a):
-        copy.start()
 
     for copy in gate_sums:
         copy.wait_recv()
@@ -437,33 +513,39 @@
     gate_second = Stage(17, gate_rows.at[2], gate_rows.at[3], z_peer, z)
     gate_first.start()
 
-    def send_back(i):
-        back = Exchange((BG, BO)[i], 2 + i, back_x.at[i], (along_xc, along_z))
-        for h in (0, 1):
-            total = part[i, 0, h].astype(F32) + near_l[i, h].astype(F32) + near_r[i, h].astype(F32)
-            total = total.astype(BF16)
-            send[2 + i, h] = total if h == 0 else dot_nn(swap_ref[...], total).astype(BF16)
-            back.first[h].start()
-        return back
-
+    to_tokens(3)
+    token_sum.left_a.start()
     sums[RG].arrived()
-    grads_back = send_back(RG)
+    for h in (0, 1):
+        total = gpart[0, h].astype(F32) + gnear_l[h].astype(F32) + gnear_r[h].astype(F32)
+        send[2, 0, :, h * (half // 2) : (h + 1) * (half // 2)] = total.astype(BF16)
+    narrow_first = Stage(BG * 4, send.at[2, 0], zbuf.at[2, 0], xc_peer, xc)
+    narrow_second = Stage(BG * 4 + 2, turned.at[2, 0], back_x.at[0, 0], z_peer, z)
+    narrow_first.start()
     gate_first.arrived()
     turn(gate_rows.at[1], gate_rows.at[2])
     gate_second.start()
-    grads_back.middle(0)
-    grads_back.middle(1)
+    narrow_first.arrived()
+    turn(zbuf.at[2, 0], turned.at[2, 0])
+    narrow_second.start()
+    to_tokens(1)
+    token_sum.right_b.start()
     sums[RO].pass_on()
+    to_tokens(2)
+    token_sum.opposite_a.start()
+    token_sum.opposite_b.start()
+    token_sum.pass_on()
     gate_second.arrived()
-    grads_back.finish(0)
-    grads_back.finish(1)
+    narrow_second.arrived()
+    token_sum.arrived()
 
     cotangent = gout_ref[...].astype(F32)
-    grad_routed, gate_grads = None, []
-    for j in (0, 1):
-        grad = gates[j] * jnp.concatenate([dot_nn(pick[j], back_x[RG, h]) for h in (0, 1)], axis=1)
-        grad_routed = grad if grad_routed is None else grad_routed + grad
-        gate_grads.append(jnp.sum(dot_nn(pick[j], gate_rows[3]), axis=-1, keepdims=True))
+    grad_routed = jnp.concatenate(
+        [gates[0] * dot_nn(pick[0, 0], back_x[0, 0]) + gates[1] * dot_nn(pick[0, 1], back_x[0, 0])]
+        + [tpart[0, h].astype(F32) + tnear_l[h].astype(F32) + tnear_r[h].astype(F32) for h in (0, 1)],
+        axis=1,
+    )
+    gate_grads = [jnp.sum(dot_nn(pick[0, j], gate_rows[3]), axis=-1, keepdims=True) for j in (0, 1)]
     gate_mean = gates[0] * gate_grads[0] + gates[1] * gate_grads[1]
     parts = [gates[j] * (gate_grads[j] - gate_mean) for j in (0, 1)]
     rest = jnp.where(first_hot, parts[0], 0.0) + jnp.where(second_hot, parts[1], 0.0)
@@ -509,7 +591,12 @@
     key_sum.opposite_b.start()
     key_sum.right_b.start()
     sums[RO].arrived()
-    outs_back = send_back(RO)
+    outs_back = Exchange(BO, 3, back_x.at[1], (along_xc, along_z))
+    for h in (0, 1):
+        total = part[0, h].astype(F32) + near_l[h].astype(F32) + near_r[h].astype(F32)
+        total = total.astype(BF16)
+        send[3, h] = total if h == 0 else dot_nn(swap_ref[...], total).astype(BF16)
+        outs_back.first[h].start()
     lax.fori_loop(0, H, key_grads, 0)
     key_sum.opposite_a.start()
     key_sum.left_a.start()
@@ -520,7 +607,7 @@
     key_sum.pass_a()
     outs_back.finish(0)
     outs_back.finish(1)
-    outs = [jnp.concatenate([dot_nn(pick[j], back_x[RO, h]) for h in (0, 1)], axis=1) for j in (0, 1)]
+    outs = [jnp.concatenate([dot_nn(pick[0, j], back_x[1, h]) for h in (0, 1)], axis=1) for j in (0, 1)]
     layer_ref[...] = (residual[...] + gates[0] * outs[0] + gates[1] * outs[1]).astype(BF16)
     key_sum.arrived()
     for h, out in ((0, gk_ref), (1, gv_ref)):
@@ -528,11 +615,11 @@
 
     for gather in (keys, grad_rows, row_gather):
         gather.sent()
-    for total in (*sums, key_sum):
+    for total in (*sums, key_sum, token_sum):
         total.sent()
-    for exchange in (grads, rows, grads_back, outs_back, gate_first, gate_second):
+    for exchange in (grads, rows, outs_back, gate_first, gate_second, narrow_first, narrow_second, *wide_first, *wide_second):
         exchange.sent()
-    for copy in gate_sums:
+    for copy in (*gate_sums, *notes):
         copy.wait_send()
 
 
@@ -592,16 +679,28 @@
             pltpu.VMEM((4, *rows), BF16),
             pltpu.VMEM((4, *rows), BF16),
             pltpu.VMEM((4, *rows), BF16),
-            pltpu.VMEM((2, tokens, SLOTS), BF16),
+            pltpu.VMEM((4, 2, tokens, SLOTS), BF16),
             pltpu.VMEM((H, tokens, 4 * block_rows), F32),
             pltpu.VMEM((tokens, width), F32),
             pltpu.VMEM((tokens, width), F32),
             pltpu.VMEM((SLOTS, hidden_units), BF16),
             pltpu.VMEM((SLOTS, hidden_units), BF16),
-            pltpu.VMEM((2, 4, *rows), BF16),
-            pltpu.VMEM((2, *rows), BF16),
-            pltpu.VMEM((2, *rows), BF16),
-            pltpu.VMEM((2, *rows), BF16),
+            pltpu.VMEM((4, *rows), BF16),
+            pltpu.VMEM(rows, BF16),
+            pltpu.VMEM(rows, BF16),
+            pltpu.VMEM(rows, BF16),
+            pltpu.VMEM((4, 2, SLOTS, half // 2), BF16),
+            pltpu.VMEM((2, SLOTS, half // 2), BF16),
+            pltpu.VMEM((2, SLOTS, half // 2), BF16),
+            pltpu.VMEM((2, SLOTS, half // 2), BF16),
+            pltpu.VMEM((4, SLOTS, half), BF16),
+            pltpu.VMEM((3, 3, SLOTS, half), BF16),
+            pltpu.VMEM((4, 2, tokens, half // 2), BF16),
+            pltpu.VMEM((2, tokens, half // 2), BF16),
+            pltpu.VMEM((2, tokens, half // 2), BF16),
+            pltpu.VMEM((2, tokens, half // 2), BF16),
+            pltpu.VMEM((2, 8, tokens), F32),
+            pltpu.VMEM((2, 3, 8, tokens), F32),
             pltpu.VMEM((4, 2, block_rows, width), BF16),
             pltpu.VMEM((2, block_rows, width), BF16),
             pltpu.VMEM((2, block_rows, width), BF16),
@@ -616,12 +715,14 @@
             pltpu.SemaphoreType.DMA((4,)),
             pltpu.SemaphoreType.DMA((18,)),
             pltpu.SemaphoreType.DMA((18,)),
-            pltpu.SemaphoreType.DMA((18,)),
-            pltpu.SemaphoreType.DMA((18,)),
-            pltpu.SemaphoreType.DMA((18,)),
-            pltpu.SemaphoreType.DMA((18,)),
+            pltpu.SemaphoreType.DMA((24,)),
+            pltpu.SemaphoreType.DMA((24,)),
+            pltpu.SemaphoreType.DMA((26,)),
+            pltpu.SemaphoreType.DMA((26,)),
             pltpu.SemaphoreType.DMA((3,)),
             pltpu.SemaphoreType.DMA((3,)),
+            pltpu.SemaphoreType.DMA((6,)),
+            pltpu.SemaphoreType.DMA((6,)),
         ],
         compiler_params=pltpu.CompilerParams(
             collective_id=0, has_side_effects=True, vmem_limit_bytes=62 * 2**20

time: 167 us -> 171 us (1.024)
  Pallas kernels: 166 us -> 168 us
    pallas_call x1, Pallas kernels: 163 us -> 165 us  [on_device(): pl.pallas_call(layer, out_shape=(shape((tokens, width), BF16), shape((tok...]
where the time goes in v4:
time: 171 us; the launch traced here: 169 us
  Pallas kernels  168 us (98%)
    pallas_call x1, Pallas kernels, on_device(): pl.pallas_call(layer, out_shape=(shape((tokens, width), BF16), shape((tok...  165 us

profile of v4, /device:TPU:1, one launch (start us, length us, event | category | flops | bytes accessed | tf_op | source)
XLA Modules:
  0.0 169.2 jit_solution(11067145059686932835)
XLA Ops:
  1.3 165.3 %layer.1 = (bf16[128,1024]{1,0:T(8,128)(2,1)}, bf16[128,1024]{1,0:T(8,128)(2,1)}, bf16[128,1024]{1,0:T(8,128)(2,1)}, f32[128,1024]{1,0:T(8,128)}, f32[128,1024]{1,0:T(8,128)}) custom-call(s32[1]{0:T(128)S(6)} %copy.17.length_ref, bf16[128,1024]{1,0:T(8,128)(2,1)} %bitcast.19, bf16[128,1024]{1,0:T(8,128)(2,1)} %bitcast.20, bf16[128,1024]{1,0:T(8,128)(2,1)} %bitcast.21, ...), custom_call_target="tpu_custom_call" | custom-call | tf_op jit(solution)/shard_map/layer/pallas_call | solution.py:649
  166.6 2.5 %hand_over.1 = (bf16[128,1024]{1,0:T(8,128)(2,1)}, bf16[128,1024]{1,0:T(8,128)(2,1)}, bf16[128,1024]{1,0:T(8,128)(2,1)}, f32[128,1024]{1,0:T(8,128)}, f32[128,1024]{1,0:T(8,128)}) custom-call(bf16[128,1024]{1,0:T(8,128)(2,1)} %get-tuple-element.15.refs_0_, bf16[128,1024]{1,0:T(8,128)(2,1)} %get-tuple-element.16.refs_1_, ...), custom_call_target="tpu_custom_call" | custom-call | tf_op jit(solution)/shard_map/hand_over/pallas_call | solution.py:746

commit v5 on v3

--- a/solution.py
+++ b/solution.py
@@ -351,7 +351,7 @@
 
         lax.fori_loop(0, hidden_units // step, up, 0)
 
-    def expert(d):
+    def rise(d):
         def up(i, carry):
             at = pl.ds(pl.multiple_of(i * step, step), step)
             weight_in = win[at, :]
@@ -365,12 +365,18 @@
             return carry
 
         lax.fori_loop(0, hidden_units // step, up, 0)
+    def fall_grads(d):
+        for n in range(width // step):
+            at = slice(n * step, (n + 1) * step)
+            h, low = divmod(n * step, half)
+            part[0, d, h, :, low : low + step] = dot_nn(ghd[...], win[:, at]).astype(BF16)
+
+    def fall_outs(d):
         gate = jnp.zeros((SLOTS, 1), F32)
         for n in range(width // step):
             at = slice(n * step, (n + 1) * step)
             h, low = divmod(n * step, half)
             inner = slice(low, low + step)
-            part[0, d, h, :, inner] = dot_nn(ghd[...], win[:, at]).astype(BF16)
             result = dot_nn(hid[...], wout[:, at])
             gate = gate + jnp.sum(result * gg[d, h, :, inner].astype(F32), axis=-1, keepdims=True)
             part[1, d, h, :, inner] = result.astype(BF16)
@@ -398,26 +404,34 @@
     prepare(1)
     own_in.wait()
 
-    expert(0)
+    rise(0)
+    fall_grads(0)
     row_gather.forward_right()
+    fall_outs(0)
     row_gather.forward_left()
     grad_rows.on_right.wait_recv()
     grad_rows.on_left.wait_recv()
     prepare(2)
     row_gather.to_right[1].wait_recv()
-    expert(3)
+    rise(3)
+    fall_grads(3)
+    sums[RG].left_a.start()
+    fall_outs(3)
     gate_sums[2].start()
-    sums[RG].left_a.start()
     row_gather.to_left[0].wait_recv()
-    expert(1)
+    rise(1)
+    fall_grads(1)
+    sums[RG].right_b.start()
+    fall_outs(1)
     gate_sums[0].start()
-    sums[RG].right_b.start()
     row_gather.on_right.wait_recv()
     row_gather.on_left.wait_recv()
-    expert(2)
-    gate_sums[1].start()
+    rise(2)
+    fall_grads(2)
     sums[RG].opposite_a.start()
     sums[RG].opposite_b.start()
+    fall_outs(2)
+    gate_sums[1].start()
     sums[RG].pass_on()
     for copy in (sums[RO].opposite_a, sums[RO].opposite_b, sums[RO].right_b, sums[RO].left_a):
         copy.start()

time: 167 us -> 166 us (level)
  Pallas kernels: 166 us -> 164 us
where the time goes in v5:
time: 166 us
  Pallas kernels  164 us (99%)
    pallas_call x1, Pallas kernels, on_device(): pl.pallas_call(layer, out_shape=(shape((tokens, width), BF16), shape((tok...  162 us

profile of v5, /device:TPU:1, one launch (start us, length us, event | category | flops | bytes accessed | tf_op | source)
XLA Modules:
  0.0 165.8 jit_solution(5492449094411024755)
XLA Ops:
  1.3 161.9 %layer.1 = (bf16[128,1024]{1,0:T(8,128)(2,1)}, bf16[128,1024]{1,0:T(8,128)(2,1)}, bf16[128,1024]{1,0:T(8,128)(2,1)}, f32[128,1024]{1,0:T(8,128)}, f32[128,1024]{1,0:T(8,128)}) custom-call(s32[1]{0:T(128)S(6)} %copy.17.length_ref, bf16[128,1024]{1,0:T(8,128)(2,1)} %bitcast.19, bf16[128,1024]{1,0:T(8,128)(2,1)} %bitcast.20, bf16[128,1024]{1,0:T(8,128)(2,1)} %bitcast.21, ...), custom_call_target="tpu_custom_call" | custom-call | tf_op jit(solution)/shard_map/layer/pallas_call | solution.py:576
  163.2 2.5 %hand_over.1 = (bf16[128,1024]{1,0:T(8,128)(2,1)}, bf16[128,1024]{1,0:T(8,128)(2,1)}, bf16[128,1024]{1,0:T(8,128)(2,1)}, f32[128,1024]{1,0:T(8,128)}, f32[128,1024]{1,0:T(8,128)}) custom-call(bf16[128,1024]{1,0:T(8,128)(2,1)} %get-tuple-element.15.refs_0_, bf16[128,1024]{1,0:T(8,128)(2,1)} %get-tuple-element.16.refs_1_, ...), custom_call_target="tpu_custom_call" | custom-call | tf_op jit(solution)/shard_map/hand_over/pallas_call | solution.py:659

commit v6 on v5

--- a/solution.py
+++ b/solution.py
@@ -530,8 +530,8 @@
     outs_back.middle(0)
     key_sum.pass_b()
     outs_back.middle(1)
+    key_sum.pass_a()
     lax.fori_loop(0, H, query_grads, 0)
-    key_sum.pass_a()
     outs_back.finish(0)
     outs_back.finish(1)
     outs = [jnp.concatenate([dot_nn(pick[j], back_x[RO, h]) for h in (0, 1)], axis=1) for j in (0, 1)]

time: 166 us -> 166 us (level)
  no operation moved by 1% of the time
where the time goes in v6:
time: 166 us
  Pallas kernels  164 us (99%)
    pallas_call x1, Pallas kernels, on_device(): pl.pallas_call(layer, out_shape=(shape((tokens, width), BF16), shape((tok...  162 us

profile of v6, /device:TPU:1, one launch (start us, length us, event | category | flops | bytes accessed | tf_op | source)
XLA Modules:
  0.0 165.8 jit_solution(6997100112590745195)
XLA Ops:
  1.3 161.9 %layer.1 = (bf16[128,1024]{1,0:T(8,128)(2,1)}, bf16[128,1024]{1,0:T(8,128)(2,1)}, bf16[128,1024]{1,0:T(8,128)(2,1)}, f32[128,1024]{1,0:T(8,128)}, f32[128,1024]{1,0:T(8,128)}) custom-call(s32[1]{0:T(128)S(6)} %copy.17.length_ref, bf16[128,1024]{1,0:T(8,128)(2,1)} %bitcast.19, bf16[128,1024]{1,0:T(8,128)(2,1)} %bitcast.20, bf16[128,1024]{1,0:T(8,128)(2,1)} %bitcast.21, ...), custom_call_target="tpu_custom_call" | custom-call | tf_op jit(solution)/shard_map/layer/pallas_call | solution.py:576
  163.2 2.5 %hand_over.1 = (bf16[128,1024]{1,0:T(8,128)(2,1)}, bf16[128,1024]{1,0:T(8,128)(2,1)}, bf16[128,1024]{1,0:T(8,128)(2,1)}, f32[128,1024]{1,0:T(8,128)}, f32[128,1024]{1,0:T(8,128)}) custom-call(bf16[128,1024]{1,0:T(8,128)(2,1)} %get-tuple-element.15.refs_0_, bf16[128,1024]{1,0:T(8,128)(2,1)} %get-tuple-element.16.refs_1_, ...), custom_call_target="tpu_custom_call" | custom-call | tf_op jit(solution)/shard_map/hand_over/pallas_call | solution.py:659
